TPU v7x, 32 devices: a whole 2x2x4 slice. The times are simulated.
32 devices in a mesh: group: 2 (over x), member: 16 (over z, y, core).
Axes of the slice: x: 2, y: 2, z: 4, core: 2. Of those that a mesh axis runs over, the one named last changes fastest.
Arguments:
- features: bfloat16 [8192, 256], P(('group', 'member')), may hold values from -6 to 6
- neighbours: int32 [8192, 10], P(('group', 'member')), may hold values from 0 to 639
- send_rows: int32 [512, 16], P(('group', 'member')), may hold values from 0 to 255
- block_counts: int32 [512], P(('group', 'member')), may hold values from 1 to 16, as said below
- hub_rows: int32 [32, 4], P(('group', 'member')), may hold values from 0 to 255
- w_self: bfloat16 [256, 256], replicated, may hold values from -0.375 to 0.375
- w_nbr: bfloat16 [256, 256], replicated, may hold values from -0.375 to 0.375
- cotangent: bfloat16 [8192, 256], P(('group', 'member')), may hold values from -6 to 6
Outputs:
- grad_self: float32 [256, 256], replicated
- grad_nbr: float32 [256, 256], replicated
- grad_features: bfloat16 [8192, 256], P(('group', 'member'))
Inputs may be any that keep to these rules, and one draw needn't show every extreme that they name: `block_counts`: entry pair of every fourth pair (pair % 4 == 0) is exactly 16.
All inputs are finite; a program needn't handle non-finite values.
Results may differ from a plain program's by a relative error of at most 0.005.
Values may be sent and summed in bfloat16 or wider, within the bound.
A program may use at most 64 MiB of HBM per device.

v0:
```python
import math

import jax
import jax.numpy as jnp
from jax import lax
from jax.sharding import PartitionSpec as P


def local(features, neighbours, send_rows, block_counts, hub_rows, w_self, w_nbr, cotangent):
    node_count, width = features.shape
    member_count = lax.axis_size("member")
    group_count = lax.axis_size("group")
    block_size = send_rows.shape[1]
    fan_count = neighbours.shape[1]
    keep_slot = jnp.arange(block_size, dtype=jnp.int32)[None, :] < block_counts[:, None]
    outgoing = jnp.where(keep_slot[:, :, None], features[send_rows], jnp.zeros((), jnp.bfloat16))
    incoming = lax.all_to_all(outgoing, "member", split_axis=0, concat_axis=0, tiled=True)
    owned_hubs = features[hub_rows.reshape(-1)]
    hub_table = lax.all_gather(owned_hubs, ("group", "member"), axis=0, tiled=True)
    table = jnp.concatenate([features, incoming.reshape(-1, width), hub_table], axis=0)
    agg_sum = jnp.zeros((node_count, width), jnp.float32)
    for sample in range(fan_count):
        agg_sum = agg_sum + table[neighbours[:, sample]].astype(jnp.float32)
    agg = (agg_sum / fan_count).astype(jnp.bfloat16)
    pre = jnp.dot(features, w_self, preferred_element_type=jnp.float32) + jnp.dot(
        agg, w_nbr, preferred_element_type=jnp.float32
    )
    sigma = jax.nn.sigmoid(pre)
    dpre = (cotangent.astype(jnp.float32) * sigma * (1.0 + pre * (1.0 - sigma))).astype(
        jnp.bfloat16
    )
    contract = (((0,), (0,)), ((), ()))
    part_self = lax.dot_general(features, dpre, contract, preferred_element_type=jnp.float32)
    part_nbr = lax.dot_general(agg, dpre, contract, preferred_element_type=jnp.float32)
    own_grad = jnp.dot(dpre, w_self.T, preferred_element_type=jnp.float32)
    dagg = jnp.dot(dpre, w_nbr.T, preferred_element_type=jnp.float32) / fan_count
    spread = jnp.zeros((table.shape[0], width), jnp.float32)
    for sample in range(fan_count):
        spread = spread.at[neighbours[:, sample]].add(dagg)
    border_stop = node_count + member_count * block_size
    border_grad = spread[node_count:border_stop].reshape(member_count, block_size, width)
    returned = lax.all_to_all(
        border_grad.astype(jnp.bfloat16), "member", split_axis=0, concat_axis=0, tiled=True
    ).astype(border_grad.dtype)
    returned = jnp.where(keep_slot[:, :, None], returned, 0.0)
    hub_grad = spread[border_stop:]
    hub_mine = lax.psum_scatter(hub_grad, ("group", "member"), scatter_dimension=0, tiled=True)
    total_grad = own_grad + spread[:node_count]
    total_grad = total_grad.at[send_rows.reshape(-1)].add(returned.reshape(-1, width))
    total_grad = total_grad.at[hub_rows.reshape(-1)].add(hub_mine)
    summed_self, summed_nbr = lax.psum((part_self, part_nbr), ("group", "member"))
    scale = 1.0 / math.sqrt(node_count * group_count * member_count)
    return (summed_self * scale, summed_nbr * scale, total_grad.astype(jnp.bfloat16))


def solution(mesh):
    in_specs = (
        P(("group", "member"), None),
        P(("group", "member"), None),
        P(("group", "member"), None),
        P(("group", "member")),
        P(("group", "member"), None),
        P(),
        P(),
        P(("group", "member"), None),
    )
    out_specs = (P(), P(), P(("group", "member"), None))
    return jax.shard_map(local, mesh=mesh, in_specs=in_specs, out_specs=out_specs, check_vma=False)
```

profile of v0, /device:TPU:0, one launch (start us, length us, event | category | flops | bytes accessed | tf_op | source)
XLA Modules:
  0.0 250.2 jit_solution(5332330522648931597)
XLA Ops:
  7.2 0.8 iota_compare_fusion
  7.9 0.7 compare_select_fusion
  8.6 0.1 reshape.104
  8.7 1.9 gather_fusion
  10.6 0.8 broadcast_select_fusion
  11.4 7.5 %all-to-all-start = ((bf16[16,16,256]{2,1,0:T(8,128)(2,1)}), bf16[16,16,256]{2,1,0:T(8,128)(2,1)S(1)}, u32[]{:S(2)}, u32[]{:S(2)}) async-start(bf16[16,16,256]{2,1,0:T(8,128)(2,1)} %broadcast_select_fusion), calls=%async_computation | async-start | bytes 262144 | tf_op jit(solution)/shard_map/all_to_all | solution.py:17
  19.1 0.6 gather_fusion.1
  19.8 42.0 %all-gather.1 = bf16[32,4,256]{2,1,0:T(4,128)(2,1)S(1)} all-gather(bf16[1,4,256]{2,1,0:T(4,128)(2,1)S(1)} %bitcast.55), channel_id=2, replica_groups=mesh['group'=2,'member'=16] {'group','member'}, dimensions={0}, use_global_device_ids=true | all-gather | bytes 67584 | tf_op jit(solution)/shard_map/all_gather | solution.py:19
  61.9 0.2 fusion.5
  62.1 1.2 gather_fusion.10
  63.3 1.2 gather_fusion.11
  64.4 1.2 gather_fusion.2
  65.6 1.2 gather_fusion.3
  66.7 1.2 gather_fusion.4
  67.9 1.2 gather_fusion.5
  69.0 1.2 gather_fusion.6
  70.2 1.2 gather_fusion.7
  71.3 1.2 gather_fusion.8
  72.5 1.2 gather_fusion.9
  73.6 0.2 multiply_convert_fusion.1
  73.8 0.7 copy-done.7
  74.5 0.3 multiply_convert_fusion
  74.8 0.2 convolution_multiply_fusion
  75.0 0.9 fusion.6
  76.0 2.1 scatter_custom_fusion
  78.1 2.2 scatter_fusion
  80.3 2.4 scatter_fusion.1
  82.7 2.2 scatter_fusion.2
  85.0 2.2 scatter_fusion.3
  87.2 2.2 scatter_fusion.4
  89.4 2.2 scatter_fusion.5
  91.7 2.2 scatter_fusion.6
  93.9 2.2 scatter_fusion.7
  96.1 2.2 scatter_fusion.8
  98.3 0.7 slice.102
  99.0 3.5 %all-to-all-start.1 = ((bf16[16,16,256]{2,1,0:T(8,128)(2,1)}), bf16[16,16,256]{2,1,0:T(8,128)(2,1)S(1)}, u32[]{:S(2)}, u32[]{:S(2)}) async-start(bf16[16,16,256]{2,1,0:T(8,128)(2,1)} %bitcast.17), calls=%async_computation.1 | async-start | bytes 262144 | tf_op jit(solution)/shard_map/all_to_all | solution.py:42
  102.6 0.9 convolution_bitcast_fusion
  103.5 0.7 slice.89
  104.2 0.2 convolution_add_fusion
  104.4 6.0 %all-to-all-done.1 = bf16[16,16,256]{2,1,0:T(8,128)(2,1)S(1)} async-done(((bf16[16,16,256]{2,1,0:T(8,128)(2,1)}), bf16[16,16,256]{2,1,0:T(8,128)(2,1)S(1)}, u32[]{:S(2)}, u32[]{:S(2)}) %all-to-all-start.1) | async-done | bytes 131104 | tf_op jit(solution)/shard_map/all_to_all | solution.py:42
  110.4 0.1 convert_select_fusion
  110.5 2.1 scatter_fusion.9
  112.6 127.1 %all-reduce.4.cloned.1.call-done = (f32[256,256]{0,1:T(8,128)}, f32[256,256]{0,1:T(8,128)}, f32[128,256]{1,0:T(8,128)}) async-done(((f32[256,256]{0,1:T(8,128)}, f32[256,256]{0,1:T(8,128)}, f32[128,256]{1,0:T(8,128)}), (f32[256,256]{0,1:T(8,128)}, f32[256,256]{0,1:T(8,128)}, f32[128,256]{1,0:T(8,128)})) %all-reduce.4.cloned.1.call-update) | async-done | bytes 655376 | tf_op jit(solution)/shard_map/psum | solution.py:51
  239.7 0.9 scatter_custom_fusion.11
  240.7 0.7 convert_element_type.64
  241.3 0.3 copy-done.3
  241.7 0.8 copy.15
  242.6 0.8 copy.16
  (38 shorter events, 0.4 us)
Async XLA Ops:
  7.2 66.7 %copy-start = (bf16[256,256]{1,0:T(8,128)(2,1)S(1)}, bf16[256,256]{1,0:T(8,128)(2,1)}, u32[]{:S(2)}) copy-start(bf16[256,256]{1,0:T(8,128)(2,1)} %param.14) | copy-start | bytes 393220
  11.4 7.5 %copy-start.5 = (s32[16,16]{1,0:T(8,128)S(1)}, s32[16,16]{1,0:T(8,128)}, u32[]{:S(2)}) copy-start(s32[16,16]{1,0:T(8,128)} %param.10) | copy-start | bytes 3076
  11.4 7.6 %copy-start.8 = (s32[1,4]{1,0:T(1,128)S(1)}, s32[1,4]{1,0:T(1,128)}, u32[]{:S(2)}) copy-start(s32[1,4]{1,0:T(1,128)} %param.12) | copy-start | bytes 52
  11.4 7.7 %copy-start.1 = (bf16[256,256]{1,0:T(8,128)(2,1)S(1)}, bf16[256,256]{1,0:T(8,128)(2,1)}, u32[]{:S(2)}) copy-start(bf16[256,256]{1,0:T(8,128)(2,1)} %param.8) | copy-start | bytes 393220
  11.4 50.7 %all-to-all-start = ((bf16[16,16,256]{2,1,0:T(8,128)(2,1)}), bf16[16,16,256]{2,1,0:T(8,128)(2,1)S(1)}, u32[]{:S(2)}, u32[]{:S(2)}) async-start(bf16[16,16,256]{2,1,0:T(8,128)(2,1)} %broadcast_select_fusion), calls=%async_computation | async-start | bytes 262144 | tf_op jit(solution)/shard_map/all_to_all | solution.py:17
  18.9 0.7 copy-start.6
  19.8 42.1 %copy-start.2 = (bf16[256,256]{1,0:T(8,128)(2,1)S(1)}, bf16[256,256]{1,0:T(8,128)(2,1)}, u32[]{:S(2)}) copy-start(bf16[256,256]{1,0:T(8,128)(2,1)} %param.13) | copy-start | bytes 393220
  73.6 0.9 copy-start.7
  99.0 11.4 %all-to-all-start.1 = ((bf16[16,16,256]{2,1,0:T(8,128)(2,1)}), bf16[16,16,256]{2,1,0:T(8,128)(2,1)S(1)}, u32[]{:S(2)}, u32[]{:S(2)}) async-start(bf16[16,16,256]{2,1,0:T(8,128)(2,1)} %bitcast.17), calls=%async_computation.1 | async-start | bytes 262144 | tf_op jit(solution)/shard_map/all_to_all | solution.py:42
  102.5 137.2 %all-reduce.4.cloned.1.call-start = ((), (), s32[]{:S(2)}) async-start(), calls=%async_computation.2 | async-start | bytes 1310720 | tf_op jit(solution)/shard_map/psum | solution.py:51
  239.7 1.6 copy-start.4
  240.7 1.0 copy-start.3
Sparse Core Ops, SparseCore 0:
  109.5 130.1 all-reduce.3
where the time goes:
time: 251 us; the launch traced here: 250 us
  waiting for transfers between devices  133 us (53%)
  blocking collectives  42 us (17%)
  other arithmetic  28.6 us (11%)
  local copies, waits for them, and re-layouts  18.2 us (7%)
  between operations  14.4 us (6%)
  starting transfers between devices  11.1 us (4%)
  matrix products  2.75 us (1%)
    psum x1, waiting for transfers between devices, local(): lax.psum((part_self, part_nbr), ('group', 'member'))  127 us
    all_gather x1, blocking collectives, local(): lax.all_gather(owned_hubs, ('group', 'member'), axis=0, tiled=True)  42 us
    scatter-add x10, other arithmetic, local(): spread = spread.at[neighbours[:, sample]].add(dagg)  22.3 us
    gather x10, local copies, waits for them, and re-layouts, local(): agg_sum = agg_sum + table[neighbours[:, sample]].astype(jnp.float32)  11.5 us
    all_to_all x1, starting transfers between devices, local(): lax.all_to_all(outgoing, 'member', split_axis=0, concat_axis=0, tiled=True)  7.52 us
    all_to_all x1, waiting for transfers between devices, local(): lax.all_to_all(border_grad.astype(jnp.bfloat16), 'member', split_axis=0,...  6 us
  transfers between devices with their start and end apart: 3, of which 2 were waited for; matrix products, arithmetic and copies ran while one was open for 2% of the time, Pallas kernels for 0%

commit v1 on v0

v1 whole, which is shorter than its diff:
```python
import functools
import math

import jax
import jax.numpy as jnp
from jax import lax
from jax.experimental import pallas as pl
from jax.experimental.pallas import tpu as pltpu
from jax.sharding import PartitionSpec as P

MESH = pl.DeviceIdType.MESH
BF = jnp.bfloat16
F32 = jnp.float32
CHUNK = 256


def dot(a, b):
    return jnp.dot(a, b, preferred_element_type=F32)


def dot_tn(a, b):
    return lax.dot_general(a, b, (((0,), (0,)), ((), ())), preferred_element_type=F32)


def dot_nt(a, b):
    return lax.dot_general(a, b, (((1,), (1,)), ((), ())), preferred_element_type=F32)


def split(value):
    high = value.astype(BF)
    return high, (value - high.astype(F32)).astype(BF)


def wait_bytes(ref, sem):
    pltpu.make_async_copy(ref, ref, sem).wait()


def kernel(
    n_group,
    n_member,
    low,
    block,
    hubs,
    feat_ref,
    nbr_ref,
    sel_ref,
    wself_ref,
    wnbr_ref,
    cot_ref,
    grad_ref,
    total_ref,
    onehot,
    out_border,
    in_border,
    out_hub,
    in_hub,
    back_border,
    ret_border,
    back_hub,
    ret_hub,
    part,
    scattered,
    mine,
    across,
    reduced,
    send_sem,
    recv_sem,
):
    nodes, width = feat_ref.shape
    half = width // 2
    fan = nbr_ref.shape[0]
    owners = n_group * n_member
    hub2 = 2 * hubs
    border_rows = n_member * block
    hub_base = nodes + border_rows
    g = lax.axis_index("group")
    m = lax.axis_index("member")
    me = g * n_member + m
    hi, lo = m // low, m % low
    n_hi = n_member // low
    n_q = n_group * low
    q = g * low + lo
    piece = mine.shape[0]

    barrier = pltpu.get_barrier_semaphore()

    def greet(step, carry):
        peer = (me + step) % owners
        pl.semaphore_signal(
            barrier, inc=1, device_id=(peer // n_member, peer % n_member), device_id_type=MESH
        )
        return carry

    lax.fori_loop(1, owners, greet, 0)

    def copy(src, dst, which, device):
        pltpu.make_async_remote_copy(
            src_ref=src,
            dst_ref=dst,
            send_sem=send_sem.at[which],
            recv_sem=recv_sem.at[which],
            device_id=device,
            device_id_type=MESH,
        ).start()

    def rows(start, count):
        return pl.ds(pl.multiple_of(start * count, count), count)

    def to_members(src, dst, which):
        def body(step, carry):
            peer = (m + step) % n_member
            copy(src.at[rows(peer, block)], dst.at[rows(m, block)], which, (g, peer))
            return carry

        lax.fori_loop(1, n_member, body, 0)

    feat = feat_ref[...]
    slots = border_rows + 128
    row_of = lax.broadcasted_iota(jnp.int32, (nodes, slots), 0)
    pick = jnp.where(row_of == sel_ref[...], 1.0, 0.0).astype(BF)
    picked = dot_tn(pick, feat)
    out_border[...] = picked[:border_rows].astype(BF)
    hub_wide = picked[border_rows : border_rows + hub2]
    lane_row = lax.broadcasted_iota(jnp.int32, (hub2, half), 0)
    out_hub[...] = jnp.where(lane_row < hubs, hub_wide[:, :half], hub_wide[:, half:])

    pl.semaphore_wait(barrier, owners - 1)

    to_members(out_border, in_border, 0)

    def send_hub(step, carry):
        peer = (me + step) % owners
        copy(out_hub, in_hub.at[rows(me, hub2)], 1, (peer // n_member, peer % n_member))
        return carry

    lax.fori_loop(1, owners, send_hub, 0)
    in_border[rows(m, block), :] = out_border[rows(m, block), :]
    in_hub[rows(me, hub2), :] = out_hub[...]

    def count(index, first):
        names = lax.broadcasted_iota(jnp.int32, (CHUNK, nodes), 0) + index * CHUNK
        if first is not None:
            names = first + (names // hub2) * hubs + names % hubs
        total = jnp.zeros((CHUNK, nodes), F32)
        for sample in range(fan):
            total = total + jnp.where(names == nbr_ref[sample : sample + 1, :], 1.0, 0.0)
        return total.astype(BF)

    plain_chunks = hub_base // CHUNK
    hub_chunks = owners * hub2 // CHUNK

    def fill_plain(index, carry):
        onehot[rows(index, CHUNK), :] = count(index, None)
        return carry

    def fill_hub(index, carry):
        onehot[rows(plain_chunks + index, CHUNK), :] = count(index, hub_base)
        return carry

    lax.fori_loop(0, plain_chunks, fill_plain, 0)
    lax.fori_loop(0, hub_chunks, fill_hub, 0)

    pre_self = dot(feat, wself_ref[...])
    agg_sum = dot_tn(onehot[:nodes, :], feat)

    others = (n_member - 1) * block
    wait_bytes(in_border.at[pl.ds(0, others)], recv_sem.at[0])
    agg_sum = agg_sum + dot_tn(onehot[nodes:hub_base, :], in_border[...])
    other_hubs = (owners - 1) * hub2
    wait_bytes(in_hub.at[pl.ds(0, other_hubs)], recv_sem.at[1])
    hub_half = lax.broadcasted_iota(jnp.int32, (owners * hub2, half), 0) % hub2 < hubs
    hub_rows = in_hub[...]
    zero = jnp.zeros((), F32)
    hub_table = jnp.concatenate(
        [jnp.where(hub_half, hub_rows, zero), jnp.where(hub_half, zero, hub_rows)], axis=1
    ).astype(BF)
    agg_sum = agg_sum + dot_tn(onehot[hub_base:, :], hub_table)
    agg = (agg_sum / fan).astype(BF)

    pre = pre_self + dot(agg, wnbr_ref[...])
    sigma = jax.nn.sigmoid(pre)
    dpre = (cot_ref[...].astype(F32) * sigma * (1.0 + pre * (1.0 - sigma))).astype(BF)

    part_self = dot_tn(feat, dpre).astype(BF)
    part_nbr = dot_tn(agg, dpre).astype(BF)
    part[0:width, :] = part_self[:, :half]
    part[width : 2 * width, :] = part_self[:, half:]
    part[2 * width : 3 * width, :] = part_nbr[:, :half]
    part[3 * width :, :] = part_nbr[:, half:]

    def near(step):
        peer = (q + step) % n_q
        return peer, (peer // low, hi * low + peer % low)

    def scatter(step, carry):
        peer, device = near(step)
        copy(part.at[rows(peer, piece)], scattered.at[rows(q, piece)], 2, device)
        return carry

    lax.fori_loop(1, n_q, scatter, 0)
    scattered[rows(q, piece), :] = part[rows(q, piece), :]

    dagg = dot_nt(dpre, wnbr_ref[...]) / fan
    dagg_high, dagg_low = split(dagg)

    def spread(start, stop):
        held = onehot[start:stop, :]
        return dot(held, dagg_high) + dot(held, dagg_low)

    back_border[...] = spread(nodes, hub_base).astype(BF)
    to_members(back_border, ret_border, 3)
    ret_border[rows(m, block), :] = back_border[rows(m, block), :]
    hub_wide = spread(hub_base, hub_base + owners * hub2)
    back_hub[...] = jnp.where(hub_half, hub_wide[:, :half], hub_wide[:, half:])

    def send_back(step, carry):
        peer = (me + step) % owners
        copy(
            back_hub.at[rows(peer, hub2)],
            ret_hub.at[rows(me, hub2)],
            4,
            (peer // n_member, peer % n_member),
        )
        return carry

    lax.fori_loop(1, owners, send_back, 0)
    ret_hub[rows(me, hub2), :] = back_hub[rows(me, hub2), :]

    wait_bytes(scattered.at[pl.ds(0, (n_q - 1) * piece)], recv_sem.at[2])
    summed = jnp.zeros((piece, half), F32)
    for index in range(n_q):
        summed = summed + scattered[index * piece : (index + 1) * piece, :].astype(F32)
    mine[...] = summed.astype(BF)

    def cross(step, carry):
        peer = (hi + step) % n_hi
        copy(mine, across.at[rows(hi, piece)], 5, (g, peer * low + lo))
        return carry

    lax.fori_loop(1, n_hi, cross, 0)
    across[rows(hi, piece), :] = mine[...]

    total = dot_nt(dpre, wself_ref[...]) + spread(0, nodes)

    wait_bytes(across.at[pl.ds(0, (n_hi - 1) * piece)], recv_sem.at[5])

    def add_up(index, carry):
        return carry + across[rows(index, piece), :].astype(F32)

    reduced[...] = lax.fori_loop(0, n_hi, add_up, jnp.zeros((piece, half), F32)).astype(BF)

    def gather(step, carry):
        _, device = near(step)
        copy(reduced, grad_ref.at[rows(q, piece)], 6, device)
        return carry

    lax.fori_loop(1, n_q, gather, 0)
    grad_ref[rows(q, piece), :] = reduced[...]

    wait_bytes(ret_border.at[pl.ds(0, others)], recv_sem.at[3])
    total = total + dot(pick[:, :border_rows], ret_border[...])
    wait_bytes(ret_hub.at[pl.ds(0, other_hubs)], recv_sem.at[4])
    hub_sum = jnp.sum(ret_hub[...].reshape(owners, hub2, half), axis=0)
    top = lane_row < hubs
    hub_sum = jnp.concatenate(
        [jnp.where(top, hub_sum, zero), jnp.where(top, zero, hub_sum)], axis=1
    )
    hub_high, hub_low = split(hub_sum)
    hub_back = jnp.concatenate(
        [
            hub_high.astype(F32),
            hub_low.astype(F32),
            jnp.zeros((128 - 2 * hub2, width), F32),
        ],
        axis=0,
    ).astype(BF)
    total_ref[...] = total + dot(pick[:, border_rows:], hub_back)

    wait_bytes(grad_ref.at[pl.ds(0, (n_q - 1) * piece)], recv_sem.at[6])
    wait_bytes(out_border.at[pl.ds(0, others)], send_sem.at[0])
    wait_bytes(in_hub.at[pl.ds(0, other_hubs)], send_sem.at[1])
    wait_bytes(part.at[pl.ds(0, (n_q - 1) * piece)], send_sem.at[2])
    wait_bytes(back_border.at[pl.ds(0, others)], send_sem.at[3])
    wait_bytes(back_hub.at[pl.ds(0, other_hubs)], send_sem.at[4])
    wait_bytes(across.at[pl.ds(0, (n_hi - 1) * piece)], send_sem.at[5])
    wait_bytes(grad_ref.at[pl.ds(0, (n_q - 1) * piece)], send_sem.at[6])


def local(features, neighbours, send_rows, block_counts, hub_rows, w_self, w_nbr, cotangent):
    nodes, width = features.shape
    n_member = lax.axis_size("member")
    n_group = lax.axis_size("group")
    block = send_rows.shape[1]
    hubs = hub_rows.shape[1]
    owners = n_group * n_member
    hub2 = 2 * hubs
    low = max(1, 8 // n_group)
    piece = 4 * width // (n_group * low)
    half = width // 2
    border_rows = n_member * block
    table_rows = nodes + border_rows + owners * hub2
    keep = jnp.arange(block, dtype=jnp.int32)[None, :] < block_counts[:, None]
    sel = jnp.concatenate(
        [
            jnp.where(keep, send_rows, -1).reshape(1, -1),
            jnp.tile(hub_rows, (1, 4)),
            jnp.full((1, 128 - 4 * hubs), -1, jnp.int32),
        ],
        axis=1,
    )
    vmem = pl.BlockSpec(memory_space=pltpu.VMEM)
    grads, total = pl.pallas_call(
        functools.partial(kernel, n_group, n_member, low, block, hubs),
        out_shape=(
            jax.ShapeDtypeStruct((4 * width, half), BF),
            jax.ShapeDtypeStruct((nodes, width), F32),
        ),
        in_specs=[vmem] * 6,
        out_specs=(vmem, vmem),
        scratch_shapes=[
            pltpu.VMEM((table_rows, nodes), BF),
            pltpu.VMEM((border_rows, width), BF),
            pltpu.VMEM((border_rows, width), BF),
            pltpu.VMEM((hub2, half), F32),
            pltpu.VMEM((owners * hub2, half), F32),
            pltpu.VMEM((border_rows, width), BF),
            pltpu.VMEM((border_rows, width), BF),
            pltpu.VMEM((owners * hub2, half), F32),
            pltpu.VMEM((owners * hub2, half), F32),
            pltpu.VMEM((4 * width, half), BF),
            pltpu.VMEM((4 * width, half), BF),
            pltpu.VMEM((piece, half), BF),
            pltpu.VMEM((n_member // low * piece, half), BF),
            pltpu.VMEM((piece, half), BF),
            pltpu.SemaphoreType.DMA((7,)),
            pltpu.SemaphoreType.DMA((7,)),
        ],
        compiler_params=pltpu.CompilerParams(
            collective_id=0, has_side_effects=True, vmem_limit_bytes=40 * 1024 * 1024
        ),
    )(features, neighbours.T, sel, w_self, w_nbr, cotangent)
    scale = 1.0 / math.sqrt(nodes * owners)
    grads = grads.astype(F32) * scale
    grad_self = jnp.concatenate([grads[:width], grads[width : 2 * width]], axis=1)
    grad_nbr = jnp.concatenate([grads[2 * width : 3 * width], grads[3 * width :]], axis=1)
    return (grad_self, grad_nbr, total.astype(BF))


def solution(mesh):
    in_specs = (
        P(("group", "member"), None),
        P(("group", "member"), None),
        P(("group", "member"), None),
        P(("group", "member")),
        P(("group", "member"), None),
        P(),
        P(),
        P(("group", "member"), None),
    )
    out_specs = (P(), P(), P(("group", "member"), None))
    return jax.shard_map(local, mesh=mesh, in_specs=in_specs, out_specs=out_specs, check_vma=False)
```

time: 251 us -> 37.8 us (0.15)
  waiting for transfers between devices: 133 us -> 0 us
  blocking collectives: 42 us -> 0 us
  Pallas kernels: 0 us -> 30.1 us
  other arithmetic: 28.6 us -> 1.62 us
  between operations: 14.4 us -> 0.7 us
  local copies, waits for them, and re-layouts: 18.2 us -> 5.04 us
  starting transfers between devices: 11.1 us -> 0 us
  matrix products: 2.75 us -> 0 us
    psum x1 -> x0, waiting for transfers between devices: 127 us -> none  [local(): lax.psum((part_self, part_nbr), ('group', 'member'))]
    all_gather x1 -> x0, blocking collectives: 42 us -> none  [local(): lax.all_gather(owned_hubs, ('group', 'member'), axis=0, tiled=True)]
    pallas_call x0 -> x1, Pallas kernels: none -> 30.1 us  [local(): pl.pallas_call(functools.partial(kernel, n_group, n_member, low, block, h...]
    scatter-add x12 -> x0, other arithmetic: 25.3 us -> none  [the longest x10 22.3 us: local(): spread = spread.at[neighbours[:, sample]].add(dagg)]
    gather x12 -> x0, local copies, waits for them, and re-layouts: 14 us -> none  [the longest x10 11.5 us: local(): agg_sum = agg_sum + table[neighbours[:, sample]].astype(jnp.float32)]
    all_to_all x2 -> x0, starting transfers between devices: 11 us -> none  [the longest x1 7.52 us: local(): lax.all_to_all(outgoing, 'member', split_axis=0, concat_axis=0, tiled=True)]
    all_to_all x2 -> x0, waiting for transfers between devices: 6 us -> none  [the longest x1 6 us: local(): lax.all_to_all(border_grad.astype(jnp.bfloat16), 'member', split_axis=0,...]
    dot_general x6 -> x0, matrix products: 2.75 us -> none  [the longest x1 0.93 us: local(): lax.dot_general(agg, dpre, contract, preferred_element_type=jnp.float32)]
  transfers between devices with their start and end apart: 3 -> 0, of which waited for: 2 -> 0; matrix products, arithmetic and copies ran while one was open for 2% -> 0% of each run, Pallas kernels for 0% -> 0%
where the time goes in v1:
time: 37.8 us; the launch traced here: 37.5 us
  Pallas kernels  30.1 us (80%)
  local copies, waits for them, and re-layouts  5.04 us (13%)
  other arithmetic  1.62 us (4%)
  between operations  0.7 us (2%)
    pallas_call x1, Pallas kernels, local(): pl.pallas_call(functools.partial(kernel, n_group, n_member, low, block, h...  30.1 us
    unnamed x16, local copies, waits for them, and re-layouts  4.76 us
    concatenate x1, other arithmetic, local(): grad_self = jnp.concatenate([grads[:width], grads[width:2 * width]], axis=1)  0.82 us

profile of v1, /device:TPU:0, one launch (start us, length us, event | category | flops | bytes accessed | tf_op | source)
XLA Modules:
  0.0 37.5 jit_solution(16758574114617932923)
XLA Ops:
  0.6 0.0 copy-start.5
  0.7 0.0 copy-start.6
  0.7 0.1 pad.6.clone
  0.7 0.6 %copy-done.6 = s32[1,4]{1,0:T(1,128)S(1)} copy-done((s32[1,4]{1,0:T(1,128)S(1)}, s32[1,4]{1,0:T(1,128)}, u32[]{:S(2)}) %copy-start.6) | copy-done | bytes 40
  1.3 0.0 copy-start.7
  1.3 0.0 copy-start.4
  1.3 0.1 tile.13
  1.4 0.0 copy-done.5
  1.4 0.6 %copy-done.7 = s32[16]{0:T(128)S(1)} copy-done((s32[16]{0:T(128)S(1)}, s32[16]{0:T(128)}, u32[]{:S(2)}) %copy-start.7) | copy-done | bytes 88
  2.0 0.1 fusion
  2.0 0.1 reshape.16
  2.1 0.0 copy-done.4
  2.1 0.0 copy-start
  2.1 0.9 %copy-done = bf16[256,256]{1,0:T(8,128)(2,1)S(1)} copy-done((bf16[256,256]{1,0:T(8,128)(2,1)S(1)}, bf16[256,256]{1,0:T(8,128)(2,1)}, u32[]{:S(2)}) %copy-start) | copy-done | bytes 131096
  3.0 0.0 copy-start.1
  3.0 0.9 %copy-done.1 = bf16[256,256]{1,0:T(8,128)(2,1)S(1)} copy-done((bf16[256,256]{1,0:T(8,128)(2,1)S(1)}, bf16[256,256]{1,0:T(8,128)(2,1)}, u32[]{:S(2)}) %copy-start.1) | copy-done | bytes 131096
  4.0 0.0 copy-start.2
  4.0 0.9 %copy-done.2 = bf16[256,256]{1,0:T(8,128)(2,1)S(1)} copy-done((bf16[256,256]{1,0:T(8,128)(2,1)S(1)}, bf16[256,256]{1,0:T(8,128)(2,1)}, u32[]{:S(2)}) %copy-start.2) | copy-done | bytes 131096
  4.9 0.0 copy-start.3
  4.9 0.9 %copy-done.3 = bf16[256,256]{1,0:T(8,128)(2,1)S(1)} copy-done((bf16[256,256]{1,0:T(8,128)(2,1)S(1)}, bf16[256,256]{1,0:T(8,128)(2,1)}, u32[]{:S(2)}) %copy-start.3) | copy-done | bytes 131096
  5.8 30.1 %shard_map.103 = (bf16[1024,128]{1,0:T(8,128)(2,1)S(1)}, f32[256,256]{1,0:T(8,128)S(1)}) custom-call(bf16[256,256]{1,0:T(8,128)(2,1)S(1)} %copy-done, s32[10,256]{1,0:T(8,128)S(1)} %bitcast.2, s32[1,384]{1,0:T(1,128)S(1)} %reshape_add_fusion.sel_ref, bf16[256,256]{1,0:T(8,128)(2,1)S(1)} %copy-done.1, bf16[256,256]{1,0:T(8,128)(2,1)S(1)} %copy-done.2, ...), custom_call_target="tpu_custom_call" | custom-call | tf_op jit(solution)/shard_map/pallas_call | solution.py:312
  35.9 0.7 %convert_element_type.7 = bf16[256,256]{1,0:T(8,128)(2,1)} convert(f32[256,256]{1,0:T(8,128)S(1)} %get-tuple-element.6) | non-fusion elementwise | flops 65536 | bytes 393216 | tf_op jit(solution)/shard_map/convert_element_type | solution.py:346
  36.7 0.8 %pad_maximum_fusion = (f32[256,256]{1,0:T(8,128)}, f32[256,256]{1,0:T(8,128)}) fusion(f32[256,128]{1,0:T(8,128)S(1)} %get-tuple-element.9, f32[256,128]{1,0:T(8,128)S(1)} %get-tuple-element.10, f32[256,128]{1,0:T(8,128)S(1)} %get-tuple-element.8, f32[256,128]{1,0:T(8,128)S(1)} %get-tuple-element.7), kind=kLoop, calls=%fused_computation.1 | loop fusion | flops 131072 | bytes 1048576 | tf_op jit(solution)/shard_map/concatenate | solution.py:344
  (5 shorter events, 0.1 us)
Async XLA Ops:
  0.6 0.8 %copy-start.5 = (s32[16,16]{1,0:T(8,128)S(1)}, s32[16,16]{1,0:T(8,128)}, u32[]{:S(2)}) copy-start(s32[16,16]{1,0:T(8,128)} %param.10) | copy-start | bytes 3076
  0.7 0.7 %copy-start.6 = (s32[1,4]{1,0:T(1,128)S(1)}, s32[1,4]{1,0:T(1,128)}, u32[]{:S(2)}) copy-start(s32[1,4]{1,0:T(1,128)} %param.12) | copy-start | bytes 52
  1.3 0.7 %copy-start.7 = (s32[16]{0:T(128)S(1)}, s32[16]{0:T(128)}, u32[]{:S(2)}) copy-start(s32[16]{0:T(128)} %param.11) | copy-start | bytes 196
  1.3 0.8 %copy-start.4 = (s32[256,10]{0,1:T(8,128)S(1)}, s32[256,10]{0,1:T(8,128)}, u32[]{:S(2)}) copy-start(s32[256,10]{0,1:T(8,128)} %param.9) | copy-start | bytes 30724
  2.1 0.9 %copy-start = (bf16[256,256]{1,0:T(8,128)(2,1)S(1)}, bf16[256,256]{1,0:T(8,128)(2,1)}, u32[]{:S(2)}) copy-start(bf16[256,256]{1,0:T(8,128)(2,1)} %feat_ref.1) | copy-start | bytes 393220
  3.0 0.9 %copy-start.1 = (bf16[256,256]{1,0:T(8,128)(2,1)S(1)}, bf16[256,256]{1,0:T(8,128)(2,1)}, u32[]{:S(2)}) copy-start(bf16[256,256]{1,0:T(8,128)(2,1)} %wself_ref.1) | copy-start | bytes 393220
  4.0 0.9 %copy-start.2 = (bf16[256,256]{1,0:T(8,128)(2,1)S(1)}, bf16[256,256]{1,0:T(8,128)(2,1)}, u32[]{:S(2)}) copy-start(bf16[256,256]{1,0:T(8,128)(2,1)} %wnbr_ref.1) | copy-start | bytes 393220
  4.9 0.9 %copy-start.3 = (bf16[256,256]{1,0:T(8,128)(2,1)S(1)}, bf16[256,256]{1,0:T(8,128)(2,1)}, u32[]{:S(2)}) copy-start(bf16[256,256]{1,0:T(8,128)(2,1)} %cot_ref.1) | copy-start | bytes 393220

commit v2 on v1

--- a/solution.py
+++ b/solution.py
@@ -35,21 +35,60 @@
     pltpu.make_async_copy(ref, ref, sem).wait()
 
 
+def select_rows(n_member, block, send_rows, counts):
+    lanes = n_member * block
+    lane = lax.broadcasted_iota(jnp.int32, (n_member, lanes), 1)
+    peer = lax.broadcasted_iota(jnp.int32, (n_member, lanes), 0)
+    own = lane // block == peer
+    slot = lax.broadcasted_iota(jnp.int32, (block, lanes), 0)
+    slot_lane = lax.broadcasted_iota(jnp.int32, (block, lanes), 1) % block
+    expand = jnp.where(slot == slot_lane, 1.0, 0.0).astype(BF)
+    spread_rows = dot(send_rows.astype(F32).astype(BF), expand)
+    row = jnp.sum(jnp.where(own, spread_rows, 0.0), axis=0, keepdims=True)
+    repeat = jnp.where(own, 1.0, 0.0).astype(BF)
+    counts = jnp.broadcast_to(counts.astype(F32), (8, n_member)).astype(BF)
+    live = dot(counts, repeat)[:1].astype(jnp.int32)
+    lane = lax.broadcasted_iota(jnp.int32, (1, lanes), 1)
+    return jnp.where(lane % block < live, row.astype(jnp.int32), -1)
+
+
+def select_hubs(hubs, hub_rows):
+    lane = lax.broadcasted_iota(jnp.int32, (hubs, 128), 1)
+    hub = lax.broadcasted_iota(jnp.int32, (hubs, 128), 0)
+    repeat = jnp.where(lane % hubs == hub, 1.0, 0.0).astype(BF)
+    wide = jnp.broadcast_to(hub_rows.astype(F32), (8, hubs)).astype(BF)
+    row = dot(wide, repeat)[:1].astype(jnp.int32)
+    lane = lax.broadcasted_iota(jnp.int32, (1, 128), 1)
+    return jnp.where(lane < 4 * hubs, row, -1)
+
+
 def kernel(
     n_group,
     n_member,
     low,
     block,
     hubs,
+    feat_hbm,
+    nbr_hbm,
+    rows_hbm,
+    counts_hbm,
+    hubs_hbm,
+    wself_hbm,
+    wnbr_hbm,
+    cot_hbm,
+    grad_ref,
+    total_ref,
     feat_ref,
     nbr_ref,
-    sel_ref,
+    rows_ref,
+    counts_ref,
+    hubs_ref,
     wself_ref,
     wnbr_ref,
     cot_ref,
-    grad_ref,
-    total_ref,
+    load_sem,
     onehot,
+    onehot_t,
     out_border,
     in_border,
     out_hub,
@@ -82,6 +121,24 @@
     q = g * low + lo
     piece = mine.shape[0]
 
+    loads = [
+        pltpu.make_async_copy(src, dst, load_sem.at[index])
+        for index, (src, dst) in enumerate(
+            (
+                (rows_hbm, rows_ref),
+                (counts_hbm, counts_ref),
+                (hubs_hbm, hubs_ref),
+                (feat_hbm, feat_ref),
+                (nbr_hbm, nbr_ref),
+                (wself_hbm, wself_ref),
+                (wnbr_hbm, wnbr_ref),
+                (cot_hbm, cot_ref),
+            )
+        )
+    ]
+    for load in loads:
+        load.start()
+
     barrier = pltpu.get_barrier_semaphore()
 
     def greet(step, carry):
@@ -114,15 +171,18 @@
 
         lax.fori_loop(1, n_member, body, 0)
 
+    for load in loads[:4]:
+        load.wait()
     feat = feat_ref[...]
-    slots = border_rows + 128
-    row_of = lax.broadcasted_iota(jnp.int32, (nodes, slots), 0)
-    pick = jnp.where(row_of == sel_ref[...], 1.0, 0.0).astype(BF)
+    sel_rows = select_rows(n_member, block, rows_ref[...], counts_ref[...])
+    sel = jnp.concatenate([sel_rows, select_hubs(hubs, hubs_ref[...])], axis=1)
+    row_of = lax.broadcasted_iota(jnp.int32, (nodes, border_rows + 128), 0)
+    pick = jnp.where(row_of == sel, 1.0, 0.0).astype(BF)
     picked = dot_tn(pick, feat)
     out_border[...] = picked[:border_rows].astype(BF)
     hub_wide = picked[border_rows : border_rows + hub2]
     lane_row = lax.broadcasted_iota(jnp.int32, (hub2, half), 0)
-    out_hub[...] = jnp.where(lane_row < hubs, hub_wide[:, :half], hub_wide[:, half:])
+    out_hub[...] = jnp.where(lane_row < hubs, hub_wide[:, :half], hub_wide[:, half:]).astype(BF)
 
     pl.semaphore_wait(barrier, owners - 1)
 
@@ -130,12 +190,15 @@
 
     def send_hub(step, carry):
         peer = (me + step) % owners
-        copy(out_hub, in_hub.at[rows(me, hub2)], 1, (peer // n_member, peer % n_member))
+        copy(out_hub, in_hub.at[me], 1, (peer // n_member, peer % n_member))
         return carry
 
     lax.fori_loop(1, owners, send_hub, 0)
     in_border[rows(m, block), :] = out_border[rows(m, block), :]
-    in_hub[rows(me, hub2), :] = out_hub[...]
+    in_hub[me] = out_hub[...]
+
+    for load in loads[4:]:
+        load.wait()
 
     def count(index, first):
         names = lax.broadcasted_iota(jnp.int32, (CHUNK, nodes), 0) + index * CHUNK
@@ -144,44 +207,49 @@
         total = jnp.zeros((CHUNK, nodes), F32)
         for sample in range(fan):
             total = total + jnp.where(names == nbr_ref[sample : sample + 1, :], 1.0, 0.0)
-        return total.astype(BF)
+        return total
 
     plain_chunks = hub_base // CHUNK
     hub_chunks = owners * hub2 // CHUNK
 
     def fill_plain(index, carry):
-        onehot[rows(index, CHUNK), :] = count(index, None)
+        total = count(index, None)
+        onehot[rows(index, CHUNK), :] = total.astype(BF)
+        onehot_t[:, rows(index, CHUNK)] = total.T.astype(BF)
         return carry
 
     def fill_hub(index, carry):
-        onehot[rows(plain_chunks + index, CHUNK), :] = count(index, hub_base)
+        total = count(index, hub_base)
+        onehot[rows(plain_chunks + index, CHUNK), :] = total.astype(BF)
+        onehot_t[:, rows(plain_chunks + index, CHUNK)] = total.T.astype(BF)
         return carry
 
     lax.fori_loop(0, plain_chunks, fill_plain, 0)
     lax.fori_loop(0, hub_chunks, fill_hub, 0)
 
     pre_self = dot(feat, wself_ref[...])
-    agg_sum = dot_tn(onehot[:nodes, :], feat)
+    agg_sum = dot(onehot_t[:, :nodes], feat)
+    feat_t = feat.astype(F32).T.astype(BF)
 
     others = (n_member - 1) * block
     wait_bytes(in_border.at[pl.ds(0, others)], recv_sem.at[0])
-    agg_sum = agg_sum + dot_tn(onehot[nodes:hub_base, :], in_border[...])
-    other_hubs = (owners - 1) * hub2
+    agg_sum = agg_sum + dot(onehot_t[:, nodes:hub_base], in_border[...])
+    other_hubs = owners - 1
     wait_bytes(in_hub.at[pl.ds(0, other_hubs)], recv_sem.at[1])
     hub_half = lax.broadcasted_iota(jnp.int32, (owners * hub2, half), 0) % hub2 < hubs
-    hub_rows = in_hub[...]
+    hub_rows = in_hub[...].astype(F32).reshape(owners * hub2, half)
     zero = jnp.zeros((), F32)
     hub_table = jnp.concatenate(
         [jnp.where(hub_half, hub_rows, zero), jnp.where(hub_half, zero, hub_rows)], axis=1
     ).astype(BF)
-    agg_sum = agg_sum + dot_tn(onehot[hub_base:, :], hub_table)
+    agg_sum = agg_sum + dot(onehot_t[:, hub_base:], hub_table)
     agg = (agg_sum / fan).astype(BF)
 
     pre = pre_self + dot(agg, wnbr_ref[...])
     sigma = jax.nn.sigmoid(pre)
     dpre = (cot_ref[...].astype(F32) * sigma * (1.0 + pre * (1.0 - sigma))).astype(BF)
 
-    part_self = dot_tn(feat, dpre).astype(BF)
+    part_self = dot(feat_t, dpre).astype(BF)
     part_nbr = dot_tn(agg, dpre).astype(BF)
     part[0:width, :] = part_self[:, :half]
     part[width : 2 * width, :] = part_self[:, half:]
@@ -211,20 +279,21 @@
     to_members(back_border, ret_border, 3)
     ret_border[rows(m, block), :] = back_border[rows(m, block), :]
     hub_wide = spread(hub_base, hub_base + owners * hub2)
-    back_hub[...] = jnp.where(hub_half, hub_wide[:, :half], hub_wide[:, half:])
+    hub_wide = jnp.where(hub_half, hub_wide[:, :half], hub_wide[:, half:])
+    back_hub[...] = hub_wide.reshape(owners, hub2, half).astype(BF)
 
     def send_back(step, carry):
         peer = (me + step) % owners
         copy(
-            back_hub.at[rows(peer, hub2)],
-            ret_hub.at[rows(me, hub2)],
+            back_hub.at[peer],
+            ret_hub.at[me],
             4,
             (peer // n_member, peer % n_member),
         )
         return carry
 
     lax.fori_loop(1, owners, send_back, 0)
-    ret_hub[rows(me, hub2), :] = back_hub[rows(me, hub2), :]
+    ret_hub[me] = back_hub[me]
 
     wait_bytes(scattered.at[pl.ds(0, (n_q - 1) * piece)], recv_sem.at[2])
     summed = jnp.zeros((piece, half), F32)
@@ -260,7 +329,7 @@
     wait_bytes(ret_border.at[pl.ds(0, others)], recv_sem.at[3])
     total = total + dot(pick[:, :border_rows], ret_border[...])
     wait_bytes(ret_hub.at[pl.ds(0, other_hubs)], recv_sem.at[4])
-    hub_sum = jnp.sum(ret_hub[...].reshape(owners, hub2, half), axis=0)
+    hub_sum = jnp.sum(ret_hub[...].astype(F32), axis=0)
     top = lane_row < hubs
     hub_sum = jnp.concatenate(
         [jnp.where(top, hub_sum, zero), jnp.where(top, zero, hub_sum)], axis=1
@@ -299,34 +368,35 @@
     half = width // 2
     border_rows = n_member * block
     table_rows = nodes + border_rows + owners * hub2
-    keep = jnp.arange(block, dtype=jnp.int32)[None, :] < block_counts[:, None]
-    sel = jnp.concatenate(
-        [
-            jnp.where(keep, send_rows, -1).reshape(1, -1),
-            jnp.tile(hub_rows, (1, 4)),
-            jnp.full((1, 128 - 4 * hubs), -1, jnp.int32),
-        ],
-        axis=1,
-    )
     vmem = pl.BlockSpec(memory_space=pltpu.VMEM)
     grads, total = pl.pallas_call(
         functools.partial(kernel, n_group, n_member, low, block, hubs),
         out_shape=(
-            jax.ShapeDtypeStruct((4 * width, half), BF),
-            jax.ShapeDtypeStruct((nodes, width), F32),
+            pltpu.VMEM((4 * width, half), BF),
+            pltpu.VMEM((nodes, width), F32),
         ),
-        in_specs=[vmem] * 6,
+        in_specs=[pl.BlockSpec(memory_space=pltpu.HBM)] * 8,
         out_specs=(vmem, vmem),
         scratch_shapes=[
+            pltpu.VMEM((nodes, width), BF),
+            pltpu.VMEM((neighbours.shape[1], nodes), jnp.int32),
+            pltpu.VMEM(send_rows.shape, jnp.int32),
+            pltpu.VMEM((1, n_member), jnp.int32),
+            pltpu.VMEM(hub_rows.shape, jnp.int32),
+            pltpu.VMEM((width, width), BF),
+            pltpu.VMEM((width, width), BF),
+            pltpu.VMEM((nodes, width), BF),
+            pltpu.SemaphoreType.DMA((8,)),
             pltpu.VMEM((table_rows, nodes), BF),
+            pltpu.VMEM((nodes, table_rows), BF),
             pltpu.VMEM((border_rows, width), BF),
             pltpu.VMEM((border_rows, width), BF),
-            pltpu.VMEM((hub2, half), F32),
-            pltpu.VMEM((owners * hub2, half), F32),
+            pltpu.VMEM((hub2, half), BF),
+            pltpu.VMEM((owners, hub2, half), BF),
             pltpu.VMEM((border_rows, width), BF),
             pltpu.VMEM((border_rows, width), BF),
-            pltpu.VMEM((owners * hub2, half), F32),
-            pltpu.VMEM((owners * hub2, half), F32),
+            pltpu.VMEM((owners, hub2, half), BF),
+            pltpu.VMEM((owners, hub2, half), BF),
             pltpu.VMEM((4 * width, half), BF),
             pltpu.VMEM((4 * width, half), BF),
             pltpu.VMEM((piece, half), BF),
@@ -336,9 +406,18 @@
             pltpu.SemaphoreType.DMA((7,)),
         ],
         compiler_params=pltpu.CompilerParams(
-            collective_id=0, has_side_effects=True, vmem_limit_bytes=40 * 1024 * 1024
+            collective_id=0, has_side_effects=True, vmem_limit_bytes=60 * 1024 * 1024
         ),
-    )(features, neighbours.T, sel, w_self, w_nbr, cotangent)
+    )(
+        features,
+        neighbours.T,
+        send_rows,
+        block_counts.reshape(1, -1),
+        hub_rows,
+        w_self,
+        w_nbr,
+        cotangent,
+    )
     scale = 1.0 / math.sqrt(nodes * owners)
     grads = grads.astype(F32) * scale
     grad_self = jnp.concatenate([grads[:width], grads[width : 2 * width]], axis=1)

time: 37.8 us -> 31.1 us (0.82)
  local copies, waits for them, and re-layouts: 5.04 us -> 0.04 us
  Pallas kernels: 30.1 us -> 28.6 us
    unnamed x16 -> x0, local copies, waits for them, and re-layouts: 4.76 us -> none
    pallas_call x1, Pallas kernels: 30.1 us -> 28.6 us  [local(): pl.pallas_call(functools.partial(kernel, n_group, n_member, low, block, h...]
where the time goes in v2:
time: 31.1 us; the launch traced here: 30.9 us
  Pallas kernels  28.6 us (92%)
  other arithmetic  1.54 us (5%)
  between operations  0.65 us (2%)
    pallas_call x1, Pallas kernels, local(): pl.pallas_call(functools.partial(kernel, n_group, n_member, low, block, h...  28.6 us
    concatenate x1, other arithmetic, local(): grad_self = jnp.concatenate([grads[:width], grads[width:2 * width]], axis=1)  0.82 us
    convert_element_type x1, other arithmetic, local(): return (grad_self, grad_nbr, total.astype(BF))  0.67 us

profile of v2, /device:TPU:0, one launch (start us, length us, event | category | flops | bytes accessed | tf_op | source)
XLA Modules:
  0.0 30.9 jit_solution(1045023459539318704)
XLA Ops:
  0.6 28.6 %shard_map.103 = (bf16[1024,128]{1,0:T(8,128)(2,1)S(1)}, f32[256,256]{1,0:T(8,128)S(1)}) custom-call(bf16[256,256]{1,0:T(8,128)(2,1)} %feat_hbm.1, s32[10,256]{1,0:T(8,128)} %bitcast.2, s32[16,16]{1,0:T(8,128)} %rows_hbm.1, s32[1,16]{1,0:T(1,128)} %bitcast.3, s32[1,4]{1,0:T(1,128)} %hubs_hbm.1, bf16[256,256]{1,0:T(8,128)(2,1)} %wself_hbm.1, ...), custom_call_target="tpu_custom_call" | custom-call | tf_op jit(solution)/shard_map/pallas_call | solution.py:372
  29.3 0.7 %convert_element_type.7 = bf16[256,256]{1,0:T(8,128)(2,1)} convert(f32[256,256]{1,0:T(8,128)S(1)} %get-tuple-element.6) | non-fusion elementwise | flops 65536 | bytes 393216 | tf_op jit(solution)/shard_map/convert_element_type | solution.py:425
  30.0 0.8 %pad_maximum_fusion = (f32[256,256]{1,0:T(8,128)}, f32[256,256]{1,0:T(8,128)}) fusion(f32[256,128]{1,0:T(8,128)S(1)} %get-tuple-element.9, f32[256,128]{1,0:T(8,128)S(1)} %get-tuple-element.10, f32[256,128]{1,0:T(8,128)S(1)} %get-tuple-element.8, f32[256,128]{1,0:T(8,128)S(1)} %get-tuple-element.7), kind=kLoop, calls=%fused_computation.1 | loop fusion | flops 131072 | bytes 1048576 | tf_op jit(solution)/shard_map/concatenate | solution.py:423
  (2 shorter events, 0.1 us)

commit v3 on v2

v3 whole, which is shorter than its diff:
```python
import functools
import math

import jax
import jax.numpy as jnp
from jax import lax
from jax.experimental import pallas as pl
from jax.experimental.pallas import tpu as pltpu
from jax.sharding import PartitionSpec as P

MESH = pl.DeviceIdType.MESH
BF = jnp.bfloat16
F32 = jnp.float32
CHUNK = 256


def dot(a, b):
    return jnp.dot(a, b, preferred_element_type=F32)


def dot_tn(a, b):
    return lax.dot_general(a, b, (((0,), (0,)), ((), ())), preferred_element_type=F32)


def dot_nt(a, b):
    return lax.dot_general(a, b, (((1,), (1,)), ((), ())), preferred_element_type=F32)


def split(value):
    high = value.astype(BF)
    return high, (value - high.astype(F32)).astype(BF)


def wait_bytes(ref, sem):
    pltpu.make_async_copy(ref, ref, sem).wait()


def select_rows(n_member, block, send_rows, counts):
    lanes = n_member * block
    lane = lax.broadcasted_iota(jnp.int32, (n_member, lanes), 1)
    peer = lax.broadcasted_iota(jnp.int32, (n_member, lanes), 0)
    own = lane // block == peer
    slot = lax.broadcasted_iota(jnp.int32, (block, lanes), 0)
    slot_lane = lax.broadcasted_iota(jnp.int32, (block, lanes), 1) % block
    expand = jnp.where(slot == slot_lane, 1.0, 0.0).astype(BF)
    spread_rows = dot(send_rows.astype(F32).astype(BF), expand)
    row = jnp.sum(jnp.where(own, spread_rows, 0.0), axis=0, keepdims=True)
    repeat = jnp.where(own, 1.0, 0.0).astype(BF)
    counts = jnp.broadcast_to(counts.astype(F32), (8, n_member)).astype(BF)
    live = dot(counts, repeat)[:1].astype(jnp.int32)
    lane = lax.broadcasted_iota(jnp.int32, (1, lanes), 1)
    return jnp.where(lane % block < live, row.astype(jnp.int32), -1)


def select_hubs(hubs, hub_rows):
    lane = lax.broadcasted_iota(jnp.int32, (hubs, 128), 1)
    hub = lax.broadcasted_iota(jnp.int32, (hubs, 128), 0)
    repeat = jnp.where(lane % hubs == hub, 1.0, 0.0).astype(BF)
    wide = jnp.broadcast_to(hub_rows.astype(F32), (8, hubs)).astype(BF)
    row = dot(wide, repeat)[:1].astype(jnp.int32)
    lane = lax.broadcasted_iota(jnp.int32, (1, 128), 1)
    return jnp.where(lane < 4 * hubs, row, -1)


def kernel(
    n_group,
    n_member,
    low,
    block,
    hubs,
    feat_hbm,
    nbr_hbm,
    rows_hbm,
    counts_hbm,
    hubs_hbm,
    wself_hbm,
    wnbr_hbm,
    cot_hbm,
    out_ref,
    feat_ref,
    nbr_ref,
    rows_ref,
    counts_ref,
    hubs_ref,
    wself_ref,
    wnbr_ref,
    cot_ref,
    load_sem,
    onehot,
    onehot_t,
    out_border,
    in_border,
    out_hub,
    line_hub,
    in_hub,
    back_border,
    ret_border,
    back_hub,
    ret_hub,
    line_back,
    line_ret,
    part,
    scattered,
    mine,
    across,
    reduced,
    send_sem,
    recv_sem,
):
    nodes, width = feat_ref.shape
    half = width // 2
    fan = nbr_ref.shape[0]
    owners = n_group * n_member
    hub2 = 2 * hubs
    border_rows = n_member * block
    hub_base = nodes + border_rows
    g = lax.axis_index("group")
    m = lax.axis_index("member")
    hi, lo = lax.div(m, low), lax.rem(m, low)
    n_hi = n_member // low
    n_q = n_group * low
    q = g * low + lo
    piece = width // n_q

    loads = [
        pltpu.make_async_copy(src, dst, load_sem.at[index])
        for index, (src, dst) in enumerate(
            (
                (rows_hbm, rows_ref),
                (counts_hbm, counts_ref),
                (hubs_hbm, hubs_ref),
                (feat_hbm, feat_ref),
                (nbr_hbm, nbr_ref),
                (wself_hbm, wself_ref),
                (wnbr_hbm, wnbr_ref),
                (cot_hbm, cot_ref),
            )
        )
    ]
    for load in loads:
        load.start()

    def loop(count, body):
        lax.fori_loop(1, count, lambda step, carry: (body(step), carry)[1], 0, unroll=count <= 16)

    def member(step):
        peer = lax.rem(m + step, n_member)
        return peer, (g, peer)

    def near(step):
        peer = lax.rem(q + step, n_q)
        return peer, (lax.div(peer, low), hi * low + lax.rem(peer, low))

    def line(step):
        peer = lax.rem(hi + step, n_hi)
        return peer, (g, peer * low + lo)

    barrier = pltpu.get_barrier_semaphore()

    def greet(device):
        pl.semaphore_signal(barrier, inc=1, device_id=device, device_id_type=MESH)

    loop(n_member, lambda step: greet(member(step)[1]))
    for step in range(1, n_group):
        for other in range(low):
            greet((lax.rem(g + step, n_group), hi * low + other))

    def copy(src, dst, which, device):
        pltpu.make_async_remote_copy(
            src_ref=src,
            dst_ref=dst,
            send_sem=send_sem.at[which],
            recv_sem=recv_sem.at[which],
            device_id=device,
            device_id_type=MESH,
        ).start()

    def rows(start, count):
        return pl.ds(pl.multiple_of(start * count, count), count)

    def to_members(src, dst, which):
        def body(step):
            peer, device = member(step)
            copy(src.at[rows(peer, block)], dst.at[rows(m, block)], which, device)

        loop(n_member, body)
        dst[rows(m, block), :] = src[rows(m, block), :]

    for load in loads[:4]:
        load.wait()
    feat = feat_ref[...]
    sel_rows = select_rows(n_member, block, rows_ref[...], counts_ref[...])
    sel = jnp.concatenate([sel_rows, select_hubs(hubs, hubs_ref[...])], axis=1)
    row_of = lax.broadcasted_iota(jnp.int32, (nodes, border_rows + 128), 0)
    pick = jnp.where(row_of == sel, 1.0, 0.0).astype(BF)
    picked = dot_tn(pick, feat)
    out_border[...] = picked[:border_rows].astype(BF)
    hub_wide = picked[border_rows : border_rows + hub2]
    lane_row = lax.broadcasted_iota(jnp.int32, (hub2, half), 0)
    out_hub[...] = jnp.where(lane_row < hubs, hub_wide[:, :half], hub_wide[:, half:]).astype(BF)

    pl.semaphore_wait(barrier, n_member - 1 + (n_group - 1) * low)

    loop(n_hi, lambda step: copy(out_hub, line_hub.at[hi], 1, line(step)[1]))
    line_hub[hi] = out_hub[...]
    to_members(out_border, in_border, 0)

    for load in loads[4:]:
        load.wait()

    def count(names):
        names = jnp.concatenate([names] * (nodes // 128), axis=1)
        total = jnp.zeros((CHUNK, nodes), F32)
        for sample in range(fan):
            total = total + jnp.where(names == nbr_ref[sample : sample + 1, :], 1.0, 0.0)
        return total

    def chunk_names(index):
        return lax.broadcasted_iota(jnp.int32, (CHUNK, 128), 0) + index * CHUNK

    def store(index, total):
        onehot[rows(index, CHUNK), :] = total.astype(BF)
        onehot_t[:, rows(index, CHUNK)] = total.T.astype(BF)

    plain_chunks = hub_base // CHUNK
    hub_chunks = owners * hub2 // CHUNK

    def fill_plain(index, carry):
        store(index, count(chunk_names(index)))
        return carry

    def fill_hub(index, carry):
        row = chunk_names(index)
        slab = lax.div(row, hub2)
        near_id = lax.div(slab, n_hi)
        owner = (
            lax.div(near_id, low) * n_member + lax.rem(slab, n_hi) * low + lax.rem(near_id, low)
        )
        store(plain_chunks + index, count(hub_base + owner * hubs + lax.rem(row, hubs)))
        return carry

    lax.fori_loop(0, plain_chunks, fill_plain, 0)

    wait_bytes(line_hub.at[pl.ds(0, n_hi - 1)], recv_sem.at[1])
    loop(n_q, lambda step: copy(line_hub, in_hub.at[q], 2, near(step)[1]))
    in_hub[q] = line_hub[...]

    lax.fori_loop(0, hub_chunks, fill_hub, 0)
    pre_self = dot(feat, wself_ref[...])
    agg_sum = dot(onehot_t[:, :nodes], feat)
    feat_t = feat.astype(F32).T.astype(BF)

    others = (n_member - 1) * block
    wait_bytes(in_border.at[pl.ds(0, others)], recv_sem.at[0])
    agg_sum = agg_sum + dot(onehot_t[:, nodes:hub_base], in_border[...])
    wait_bytes(in_hub.at[pl.ds(0, n_q - 1)], recv_sem.at[2])
    hub_half = lax.broadcasted_iota(jnp.int32, (owners * hub2, half), 0) % hub2 < hubs
    hub_rows = in_hub[...].astype(F32).reshape(owners * hub2, half)
    zero = jnp.zeros((), F32)
    hub_table = jnp.concatenate(
        [jnp.where(hub_half, hub_rows, zero), jnp.where(hub_half, zero, hub_rows)], axis=1
    ).astype(BF)
    agg_sum = agg_sum + dot(onehot_t[:, hub_base:], hub_table)
    agg = (agg_sum / fan).astype(BF)

    pre = pre_self + dot(agg, wnbr_ref[...])
    sigma = jax.nn.sigmoid(pre)
    dpre = (cot_ref[...].astype(F32) * sigma * (1.0 + pre * (1.0 - sigma))).astype(BF)

    def scatter(which):
        def body(step):
            peer, device = near(step)
            copy(
                part.at[rows(which * n_q + peer, piece)],
                scattered.at[rows(which * n_q + q, piece)],
                3 + which,
                device,
            )

        loop(n_q, body)
        own = rows(which * n_q + q, piece)
        scattered[own, :] = part[own, :]

    part[:width, :] = dot(feat_t, dpre).astype(BF)
    scatter(0)
    part[width:, :] = dot_tn(agg, dpre).astype(BF)
    scatter(1)

    dagg = dot_nt(dpre, wnbr_ref[...]) / fan
    dagg_high, dagg_low = split(dagg)

    def spread(start, stop):
        held = onehot[start:stop, :]
        return dot(held, dagg_high) + dot(held, dagg_low)

    hub_wide = spread(hub_base, hub_base + owners * hub2)
    hub_wide = jnp.where(hub_half, hub_wide[:, :half], hub_wide[:, half:])
    back_hub[...] = hub_wide.reshape(n_q, n_hi, hub2, half).astype(BF)

    def send_back(step):
        peer, device = near(step)
        copy(back_hub.at[peer], ret_hub.at[q], 10, device)

    loop(n_q, send_back)
    ret_hub[q] = back_hub[q]
    back_border[...] = spread(nodes, hub_base).astype(BF)
    to_members(back_border, ret_border, 9)

    near_rows = (n_q - 1) * piece
    line_rows = (n_hi - 1) * piece

    def cross(which):
        wait_bytes(scattered.at[pl.ds(which * width, near_rows)], recv_sem.at[3 + which])
        summed = jnp.zeros((piece, width), F32)
        for index in range(n_q):
            start = which * width + index * piece
            summed = summed + scattered[start : start + piece, :].astype(F32)
        source = mine.at[pl.ds(which * piece, piece)]
        source[...] = summed.astype(BF)
        slot = rows(which * n_hi + hi, piece)
        loop(n_hi, lambda step: copy(source, across.at[slot], 5 + which, line(step)[1]))
        across[slot, :] = source[...]

    cross(0)
    cross(1)

    total = dot_nt(dpre, wself_ref[...]) + spread(0, nodes)

    wait_bytes(ret_hub.at[pl.ds(0, n_q - 1)], recv_sem.at[10])
    line_back[...] = jnp.sum(ret_hub[...].astype(F32), axis=0).astype(BF)

    def send_line(step):
        peer, device = line(step)
        copy(line_back.at[peer], line_ret.at[hi], 11, device)

    loop(n_hi, send_line)
    line_ret[hi] = line_back[hi]

    def gather(which):
        first = which * n_hi
        wait_bytes(across.at[pl.ds(first * piece, line_rows)], recv_sem.at[5 + which])
        summed = lax.fori_loop(
            0,
            n_hi,
            lambda index, carry: carry + across[rows(first + index, piece), :].astype(F32),
            jnp.zeros((piece, width), F32),
            unroll=n_hi <= 16,
        )
        source = reduced.at[pl.ds(which * piece, piece)]
        source[...] = summed.astype(BF)
        slot = rows(which * n_q + q, piece)
        loop(n_q, lambda step: copy(source, out_ref.at[slot], 7 + which, near(step)[1]))
        out_ref[slot, :] = source[...]

    gather(0)
    gather(1)

    wait_bytes(ret_border.at[pl.ds(0, others)], recv_sem.at[9])
    total = total + dot(pick[:, :border_rows], ret_border[...])
    wait_bytes(line_ret.at[pl.ds(0, n_hi - 1)], recv_sem.at[11])
    hub_sum = jnp.sum(line_ret[...].astype(F32), axis=0)
    top = lane_row < hubs
    hub_sum = jnp.concatenate(
        [jnp.where(top, hub_sum, zero), jnp.where(top, zero, hub_sum)], axis=1
    )
    hub_high, hub_low = split(hub_sum)
    hub_back = jnp.concatenate(
        [
            hub_high.astype(F32),
            hub_low.astype(F32),
            jnp.zeros((128 - 2 * hub2, width), F32),
        ],
        axis=0,
    ).astype(BF)
    out_ref[2 * width :, :] = (total + dot(pick[:, border_rows:], hub_back)).astype(BF)

    wait_bytes(out_border.at[pl.ds(0, others)], send_sem.at[0])
    wait_bytes(line_hub.at[pl.ds(0, n_hi - 1)], send_sem.at[1])
    wait_bytes(in_hub.at[pl.ds(0, n_q - 1)], send_sem.at[2])
    wait_bytes(back_border.at[pl.ds(0, others)], send_sem.at[9])
    wait_bytes(back_hub.at[pl.ds(0, n_q - 1)], send_sem.at[10])
    wait_bytes(line_back.at[pl.ds(0, n_hi - 1)], send_sem.at[11])
    for which in range(2):
        wait_bytes(part.at[pl.ds(which * width, near_rows)], send_sem.at[3 + which])
        wait_bytes(across.at[pl.ds(which * n_hi * piece, line_rows)], send_sem.at[5 + which])
    for which in range(2):
        wait_bytes(out_ref.at[pl.ds(which * width, near_rows)], recv_sem.at[7 + which])
        wait_bytes(part.at[pl.ds(which * width, near_rows)], send_sem.at[7 + which])


def local(features, neighbours, send_rows, block_counts, hub_rows, w_self, w_nbr, cotangent):
    nodes, width = features.shape
    n_member = lax.axis_size("member")
    n_group = lax.axis_size("group")
    block = send_rows.shape[1]
    hubs = hub_rows.shape[1]
    owners = n_group * n_member
    hub2 = 2 * hubs
    low = max(1, 8 // n_group)
    n_q = n_group * low
    n_hi = n_member // low
    piece = width // n_q
    half = width // 2
    border_rows = n_member * block
    table_rows = nodes + border_rows + owners * hub2
    border = pltpu.VMEM((border_rows, width), BF)
    hub_line = pltpu.VMEM((n_hi, hub2, half), BF)
    hub_all = pltpu.VMEM((n_q, n_hi, hub2, half), BF)
    pair = pltpu.VMEM((2 * width, width), BF)
    result = pl.pallas_call(
        functools.partial(kernel, n_group, n_member, low, block, hubs),
        out_shape=pltpu.VMEM((2 * width + nodes, width), BF),
        in_specs=[pl.BlockSpec(memory_space=pltpu.HBM)] * 8,
        out_specs=pl.BlockSpec(memory_space=pltpu.VMEM),
        scratch_shapes=[
            pltpu.VMEM((nodes, width), BF),
            pltpu.VMEM((neighbours.shape[1], nodes), jnp.int32),
            pltpu.VMEM(send_rows.shape, jnp.int32),
            pltpu.VMEM((1, n_member), jnp.int32),
            pltpu.VMEM(hub_rows.shape, jnp.int32),
            pltpu.VMEM((width, width), BF),
            pltpu.VMEM((width, width), BF),
            pltpu.VMEM((nodes, width), BF),
            pltpu.SemaphoreType.DMA((8,)),
            pltpu.VMEM((table_rows, nodes), BF),
            pltpu.VMEM((nodes, table_rows), BF),
            border,
            border,
            pltpu.VMEM((hub2, half), BF),
            hub_line,
            hub_all,
            border,
            border,
            hub_all,
            hub_all,
            hub_line,
            hub_line,
            pair,
            pair,
            pltpu.VMEM((2 * piece, width), BF),
            pltpu.VMEM((2 * n_hi * piece, width), BF),
            pltpu.VMEM((2 * piece, width), BF),
            pltpu.SemaphoreType.DMA((12,)),
            pltpu.SemaphoreType.DMA((12,)),
        ],
        compiler_params=pltpu.CompilerParams(
            collective_id=0, has_side_effects=True, vmem_limit_bytes=60 * 1024 * 1024
        ),
    )(
        features,
        neighbours.T,
        send_rows,
        block_counts.reshape(1, -1),
        hub_rows,
        w_self,
        w_nbr,
        cotangent,
    )
    scale = 1.0 / math.sqrt(nodes * owners)
    grad_self = result[:width].astype(F32) * scale
    grad_nbr = result[width : 2 * width].astype(F32) * scale
    return (grad_self, grad_nbr, result[2 * width :])


def solution(mesh):
    in_specs = (
        P(("group", "member"), None),
        P(("group", "member"), None),
        P(("group", "member"), None),
        P(("group", "member")),
        P(("group", "member"), None),
        P(),
        P(),
        P(("group", "member"), None),
    )
    out_specs = (P(), P(), P(("group", "member"), None))
    return jax.shard_map(local, mesh=mesh, in_specs=in_specs, out_specs=out_specs, check_vma=False)
```

time: 31.1 us -> 29.2 us (0.939)
  Pallas kernels: 28.6 us -> 26.8 us
  other arithmetic: 1.54 us -> 0.83 us
  local copies, waits for them, and re-layouts: 0.04 us -> 0.66 us
    pallas_call x1, Pallas kernels: 28.6 us -> 26.8 us  [local(): pl.pallas_call(functools.partial(kernel, n_group, n_member, low, block, h...]
    concatenate x1 -> x0, other arithmetic: 0.82 us -> none  [local(): grad_self = jnp.concatenate([grads[:width], grads[width:2 * width]], axis=1)]
    mul x1, other arithmetic: 0.04 us -> 0.83 us  [local(): grad_nbr = result[width:2 * width].astype(F32) * scale]
    convert_element_type x1 -> x0, other arithmetic: 0.67 us -> none  [local(): return (grad_self, grad_nbr, total.astype(BF))]
    slice x1, local copies, waits for them, and re-layouts: 0.04 us -> 0.66 us  [local(): return (grad_self, grad_nbr, result[2 * width:])]
where the time goes in v3:
time: 29.2 us; the launch traced here: 29 us
  Pallas kernels  26.8 us (92%)
  other arithmetic  0.83 us (3%)
  local copies, waits for them, and re-layouts  0.66 us (2%)
  between operations  0.64 us (2%)
    pallas_call x1, Pallas kernels, local(): pl.pallas_call(functools.partial(kernel, n_group, n_member, low, block, h...  26.8 us
    mul x1, other arithmetic, local(): grad_nbr = result[width:2 * width].astype(F32) * scale  0.83 us
    slice x1, local copies, waits for them, and re-layouts, local(): return (grad_self, grad_nbr, result[2 * width:])  0.66 us

profile of v3, /device:TPU:0, one launch (start us, length us, event | category | flops | bytes accessed | tf_op | source)
XLA Modules:
  0.0 29.0 jit_solution(1852636936090554743)
XLA Ops:
  0.6 26.8 %shard_map.103 = bf16[768,256]{1,0:T(8,128)(2,1)S(1)} custom-call(bf16[256,256]{1,0:T(8,128)(2,1)} %feat_hbm.1, s32[10,256]{1,0:T(8,128)} %bitcast.2, s32[16,16]{1,0:T(8,128)} %rows_hbm.1, s32[1,16]{1,0:T(1,128)} %bitcast.3, s32[1,4]{1,0:T(1,128)} %hubs_hbm.1, bf16[256,256]{1,0:T(8,128)(2,1)} %wself_hbm.1, bf16[256,256]{1,0:T(8,128)(2,1)} %wnbr_hbm.1, ...), custom_call_target="tpu_custom_call" | custom-call | tf_op jit(solution)/shard_map/pallas_call | solution.py:410
  27.5 0.8 %convert_multiply_fusion = (f32[256,256]{1,0:T(8,128)}, f32[256,256]{1,0:T(8,128)}) fusion(bf16[768,256]{1,0:T(8,128)(2,1)S(1)} %shard_map.103), kind=kLoop, calls=%fused_computation | loop fusion | flops 262144 | bytes 786432 | tf_op jit(solution)/shard_map/mul | solution.py:461
  28.3 0.7 %slice.11 = bf16[256,256]{1,0:T(8,128)(2,1)} slice(bf16[768,256]{1,0:T(8,128)(2,1)S(1)} %shard_map.103), slice={[512:768], [0:256]} | slice | bytes 262144 | tf_op jit(solution)/shard_map/slice | solution.py:462

commit v4 on v3

--- a/solution.py
+++ b/solution.py
@@ -12,6 +12,10 @@
 BF = jnp.bfloat16
 F32 = jnp.float32
 CHUNK = 256
+CUTS = 4
+BORDER, HUB_LINE, HUB_NEAR, BACK_BORDER, BACK_NEAR, BACK_LINE = range(6)
+SCATTER, CROSS, GATHER = 6, 6 + CUTS, 6 + 2 * CUTS
+SEMS = 6 + 3 * CUTS
 
 
 def dot(a, b):
@@ -120,7 +124,8 @@
     n_hi = n_member // low
     n_q = n_group * low
     q = g * low + lo
-    piece = width // n_q
+    piece = 2 * width // (CUTS * n_q)
+    cut = n_q * piece
 
     loads = [
         pltpu.make_async_copy(src, dst, load_sem.at[index])
@@ -186,13 +191,14 @@
         loop(n_member, body)
         dst[rows(m, block), :] = src[rows(m, block), :]
 
-    for load in loads[:4]:
+    for load in loads[:3]:
         load.wait()
-    feat = feat_ref[...]
     sel_rows = select_rows(n_member, block, rows_ref[...], counts_ref[...])
     sel = jnp.concatenate([sel_rows, select_hubs(hubs, hubs_ref[...])], axis=1)
     row_of = lax.broadcasted_iota(jnp.int32, (nodes, border_rows + 128), 0)
     pick = jnp.where(row_of == sel, 1.0, 0.0).astype(BF)
+    loads[3].wait()
+    feat = feat_ref[...]
     picked = dot_tn(pick, feat)
     out_border[...] = picked[:border_rows].astype(BF)
     hub_wide = picked[border_rows : border_rows + hub2]
@@ -201,9 +207,9 @@
 
     pl.semaphore_wait(barrier, n_member - 1 + (n_group - 1) * low)
 
-    loop(n_hi, lambda step: copy(out_hub, line_hub.at[hi], 1, line(step)[1]))
+    loop(n_hi, lambda step: copy(out_hub, line_hub.at[hi], HUB_LINE, line(step)[1]))
     line_hub[hi] = out_hub[...]
-    to_members(out_border, in_border, 0)
+    to_members(out_border, in_border, BORDER)
 
     for load in loads[4:]:
         load.wait()
@@ -239,21 +245,19 @@
         store(plain_chunks + index, count(hub_base + owner * hubs + lax.rem(row, hubs)))
         return carry
 
-    lax.fori_loop(0, plain_chunks, fill_plain, 0)
-
-    wait_bytes(line_hub.at[pl.ds(0, n_hi - 1)], recv_sem.at[1])
-    loop(n_q, lambda step: copy(line_hub, in_hub.at[q], 2, near(step)[1]))
+    fill_plain(0, 0)
+
+    wait_bytes(line_hub.at[pl.ds(0, n_hi - 1)], recv_sem.at[HUB_LINE])
+    loop(n_q, lambda step: copy(line_hub, in_hub.at[q], HUB_NEAR, near(step)[1]))
     in_hub[q] = line_hub[...]
 
+    lax.fori_loop(1, plain_chunks, fill_plain, 0)
     lax.fori_loop(0, hub_chunks, fill_hub, 0)
     pre_self = dot(feat, wself_ref[...])
     agg_sum = dot(onehot_t[:, :nodes], feat)
     feat_t = feat.astype(F32).T.astype(BF)
 
-    others = (n_member - 1) * block
-    wait_bytes(in_border.at[pl.ds(0, others)], recv_sem.at[0])
-    agg_sum = agg_sum + dot(onehot_t[:, nodes:hub_base], in_border[...])
-    wait_bytes(in_hub.at[pl.ds(0, n_q - 1)], recv_sem.at[2])
+    wait_bytes(in_hub.at[pl.ds(0, n_q - 1)], recv_sem.at[HUB_NEAR])
     hub_half = lax.broadcasted_iota(jnp.int32, (owners * hub2, half), 0) % hub2 < hubs
     hub_rows = in_hub[...].astype(F32).reshape(owners * hub2, half)
     zero = jnp.zeros((), F32)
@@ -261,10 +265,13 @@
         [jnp.where(hub_half, hub_rows, zero), jnp.where(hub_half, zero, hub_rows)], axis=1
     ).astype(BF)
     agg_sum = agg_sum + dot(onehot_t[:, hub_base:], hub_table)
-    agg = (agg_sum / fan).astype(BF)
+    others = (n_member - 1) * block
+    wait_bytes(in_border.at[pl.ds(0, others)], recv_sem.at[BORDER])
+    agg_sum = agg_sum + dot(onehot_t[:, nodes:hub_base], in_border[...])
+    agg = (agg_sum * (1.0 / fan)).astype(BF)
 
     pre = pre_self + dot(agg, wnbr_ref[...])
-    sigma = jax.nn.sigmoid(pre)
+    sigma = 0.5 * jnp.tanh(0.5 * pre) + 0.5
     dpre = (cot_ref[...].astype(F32) * sigma * (1.0 + pre * (1.0 - sigma))).astype(BF)
 
     def scatter(which):
@@ -273,7 +280,7 @@
             copy(
                 part.at[rows(which * n_q + peer, piece)],
                 scattered.at[rows(which * n_q + q, piece)],
-                3 + which,
+                SCATTER + which,
                 device,
             )
 
@@ -281,12 +288,20 @@
         own = rows(which * n_q + q, piece)
         scattered[own, :] = part[own, :]
 
-    part[:width, :] = dot(feat_t, dpre).astype(BF)
-    scatter(0)
-    part[width:, :] = dot_tn(agg, dpre).astype(BF)
-    scatter(1)
-
-    dagg = dot_nt(dpre, wnbr_ref[...]) / fan
+    per = width // cut
+    for which in range(per):
+        span = slice(which * cut, (which + 1) * cut)
+        part[span, :] = dot(feat_t[span, :], dpre).astype(BF)
+        scatter(which)
+    agg_t = agg.astype(F32).T.astype(BF)
+    for which in range(per):
+        span = slice(which * cut, (which + 1) * cut)
+        part[width + which * cut : width + (which + 1) * cut, :] = dot(
+            agg_t[span, :], dpre
+        ).astype(BF)
+        scatter(per + which)
+
+    dagg = dot_nt(dpre, wnbr_ref[...]) * (1.0 / fan)
     dagg_high, dagg_low = split(dagg)
 
     def spread(start, stop):
@@ -299,46 +314,46 @@
 
     def send_back(step):
         peer, device = near(step)
-        copy(back_hub.at[peer], ret_hub.at[q], 10, device)
+        copy(back_hub.at[peer], ret_hub.at[q], BACK_NEAR, device)
 
     loop(n_q, send_back)
     ret_hub[q] = back_hub[q]
     back_border[...] = spread(nodes, hub_base).astype(BF)
-    to_members(back_border, ret_border, 9)
+    to_members(back_border, ret_border, BACK_BORDER)
 
     near_rows = (n_q - 1) * piece
     line_rows = (n_hi - 1) * piece
 
     def cross(which):
-        wait_bytes(scattered.at[pl.ds(which * width, near_rows)], recv_sem.at[3 + which])
+        wait_bytes(scattered.at[pl.ds(which * cut, near_rows)], recv_sem.at[SCATTER + which])
         summed = jnp.zeros((piece, width), F32)
         for index in range(n_q):
-            start = which * width + index * piece
+            start = which * cut + index * piece
             summed = summed + scattered[start : start + piece, :].astype(F32)
         source = mine.at[pl.ds(which * piece, piece)]
         source[...] = summed.astype(BF)
         slot = rows(which * n_hi + hi, piece)
-        loop(n_hi, lambda step: copy(source, across.at[slot], 5 + which, line(step)[1]))
+        loop(n_hi, lambda step: copy(source, across.at[slot], CROSS + which, line(step)[1]))
         across[slot, :] = source[...]
 
-    cross(0)
-    cross(1)
+    for which in range(CUTS):
+        cross(which)
 
     total = dot_nt(dpre, wself_ref[...]) + spread(0, nodes)
 
-    wait_bytes(ret_hub.at[pl.ds(0, n_q - 1)], recv_sem.at[10])
+    wait_bytes(ret_hub.at[pl.ds(0, n_q - 1)], recv_sem.at[BACK_NEAR])
     line_back[...] = jnp.sum(ret_hub[...].astype(F32), axis=0).astype(BF)
 
     def send_line(step):
         peer, device = line(step)
-        copy(line_back.at[peer], line_ret.at[hi], 11, device)
+        copy(line_back.at[peer], line_ret.at[hi], BACK_LINE, device)
 
     loop(n_hi, send_line)
     line_ret[hi] = line_back[hi]
 
     def gather(which):
         first = which * n_hi
-        wait_bytes(across.at[pl.ds(first * piece, line_rows)], recv_sem.at[5 + which])
+        wait_bytes(across.at[pl.ds(first * piece, line_rows)], recv_sem.at[CROSS + which])
         summed = lax.fori_loop(
             0,
             n_hi,
@@ -349,15 +364,15 @@
         source = reduced.at[pl.ds(which * piece, piece)]
         source[...] = summed.astype(BF)
         slot = rows(which * n_q + q, piece)
-        loop(n_q, lambda step: copy(source, out_ref.at[slot], 7 + which, near(step)[1]))
+        loop(n_q, lambda step: copy(source, out_ref.at[slot], GATHER + which, near(step)[1]))
         out_ref[slot, :] = source[...]
 
-    gather(0)
-    gather(1)
-
-    wait_bytes(ret_border.at[pl.ds(0, others)], recv_sem.at[9])
+    for which in range(CUTS):
+        gather(which)
+
+    wait_bytes(ret_border.at[pl.ds(0, others)], recv_sem.at[BACK_BORDER])
     total = total + dot(pick[:, :border_rows], ret_border[...])
-    wait_bytes(line_ret.at[pl.ds(0, n_hi - 1)], recv_sem.at[11])
+    wait_bytes(line_ret.at[pl.ds(0, n_hi - 1)], recv_sem.at[BACK_LINE])
     hub_sum = jnp.sum(line_ret[...].astype(F32), axis=0)
     top = lane_row < hubs
     hub_sum = jnp.concatenate(
@@ -374,18 +389,31 @@
     ).astype(BF)
     out_ref[2 * width :, :] = (total + dot(pick[:, border_rows:], hub_back)).astype(BF)
 
-    wait_bytes(out_border.at[pl.ds(0, others)], send_sem.at[0])
-    wait_bytes(line_hub.at[pl.ds(0, n_hi - 1)], send_sem.at[1])
-    wait_bytes(in_hub.at[pl.ds(0, n_q - 1)], send_sem.at[2])
-    wait_bytes(back_border.at[pl.ds(0, others)], send_sem.at[9])
-    wait_bytes(back_hub.at[pl.ds(0, n_q - 1)], send_sem.at[10])
-    wait_bytes(line_back.at[pl.ds(0, n_hi - 1)], send_sem.at[11])
-    for which in range(2):
-        wait_bytes(part.at[pl.ds(which * width, near_rows)], send_sem.at[3 + which])
-        wait_bytes(across.at[pl.ds(which * n_hi * piece, line_rows)], send_sem.at[5 + which])
-    for which in range(2):
-        wait_bytes(out_ref.at[pl.ds(which * width, near_rows)], recv_sem.at[7 + which])
-        wait_bytes(part.at[pl.ds(which * width, near_rows)], send_sem.at[7 + which])
+    wait_bytes(out_border.at[pl.ds(0, others)], send_sem.at[BORDER])
+    wait_bytes(line_hub.at[pl.ds(0, n_hi - 1)], send_sem.at[HUB_LINE])
+    wait_bytes(in_hub.at[pl.ds(0, n_q - 1)], send_sem.at[HUB_NEAR])
+    wait_bytes(back_border.at[pl.ds(0, others)], send_sem.at[BACK_BORDER])
+    wait_bytes(back_hub.at[pl.ds(0, n_q - 1)], send_sem.at[BACK_NEAR])
+    wait_bytes(line_back.at[pl.ds(0, n_hi - 1)], send_sem.at[BACK_LINE])
+    for which in range(CUTS):
+        wait_bytes(part.at[pl.ds(which * cut, near_rows)], send_sem.at[SCATTER + which])
+        wait_bytes(across.at[pl.ds(which * n_hi * piece, line_rows)], send_sem.at[CROSS + which])
+    for which in range(CUTS):
+        wait_bytes(out_ref.at[pl.ds(which * cut, near_rows)], recv_sem.at[GATHER + which])
+        wait_bytes(part.at[pl.ds(which * cut, near_rows)], send_sem.at[GATHER + which])
+
+
+def finish(scale, held_ref, self_hbm, nbr_hbm, feat_hbm, stage, sems):
+    width = stage.shape[0] // 2
+    copies = [pltpu.make_async_copy(held_ref.at[pl.ds(2 * width, feat_hbm.shape[0])], feat_hbm, sems.at[2])]
+    copies[0].start()
+    for index, target in enumerate((self_hbm, nbr_hbm)):
+        span = pl.ds(index * width, width)
+        stage[span, :] = held_ref[span, :].astype(F32) * scale
+        copies.append(pltpu.make_async_copy(stage.at[span], target, sems.at[index]))
+        copies[-1].start()
+    for copy in copies:
+        copy.wait()
 
 
 def local(features, neighbours, send_rows, block_counts, hub_rows, w_self, w_nbr, cotangent):
@@ -399,7 +427,7 @@
     low = max(1, 8 // n_group)
     n_q = n_group * low
     n_hi = n_member // low
-    piece = width // n_q
+    piece = 2 * width // (CUTS * n_q)
     half = width // 2
     border_rows = n_member * block
     table_rows = nodes + border_rows + owners * hub2
@@ -437,11 +465,11 @@
             hub_line,
             pair,
             pair,
-            pltpu.VMEM((2 * piece, width), BF),
-            pltpu.VMEM((2 * n_hi * piece, width), BF),
-            pltpu.VMEM((2 * piece, width), BF),
-            pltpu.SemaphoreType.DMA((12,)),
-            pltpu.SemaphoreType.DMA((12,)),
+            pltpu.VMEM((CUTS * piece, width), BF),
+            pltpu.VMEM((CUTS * n_hi * piece, width), BF),
+            pltpu.VMEM((CUTS * piece, width), BF),
+            pltpu.SemaphoreType.DMA((SEMS,)),
+            pltpu.SemaphoreType.DMA((SEMS,)),
         ],
         compiler_params=pltpu.CompilerParams(
             collective_id=0, has_side_effects=True, vmem_limit_bytes=60 * 1024 * 1024
@@ -457,9 +485,14 @@
         cotangent,
     )
     scale = 1.0 / math.sqrt(nodes * owners)
-    grad_self = result[:width].astype(F32) * scale
-    grad_nbr = result[width : 2 * width].astype(F32) * scale
-    return (grad_self, grad_nbr, result[2 * width :])
+    full = jax.ShapeDtypeStruct((width, width), F32)
+    return pl.pallas_call(
+        functools.partial(finish, scale),
+        out_shape=(full, full, jax.ShapeDtypeStruct((nodes, width), BF)),
+        in_specs=[pl.BlockSpec(memory_space=pltpu.VMEM)],
+        out_specs=(pl.BlockSpec(memory_space=pl.ANY),) * 3,
+        scratch_shapes=[pltpu.VMEM((2 * width, width), F32), pltpu.SemaphoreType.DMA((3,))],
+    )(result)
 
 
 def solution(mesh):

time: 29.2 us -> 30.3 us (1.038)
  Pallas kernels: 26.8 us -> 28.7 us
  other arithmetic: 0.83 us -> 0 us
    pallas_call x0 -> x1, Pallas kernels: none -> 1.85 us  [local(): pl.pallas_call(functools.partial(finish, scale), out_shape=(full, full, j...]
    mul x1 -> x0, other arithmetic: 0.83 us -> none  [local(): grad_nbr = result[width:2 * width].astype(F32) * scale]
    unnamed x0 -> x2, local copies, waits for them, and re-layouts: none -> 0.73 us
    slice x1 -> x0, local copies, waits for them, and re-layouts: 0.66 us -> none  [local(): return (grad_self, grad_nbr, result[2 * width:])]
where the time goes in v4:
time: 30.3 us; the launch traced here: 30.1 us
  Pallas kernels  28.7 us (95%)
  local copies, waits for them, and re-layouts  0.73 us (2%)
  between operations  0.65 us (2%)
    pallas_call x1, Pallas kernels, local(): pl.pallas_call(functools.partial(kernel, n_group, n_member, low, block, h...  26.9 us
    pallas_call x1, Pallas kernels, local(): pl.pallas_call(functools.partial(finish, scale), out_shape=(full, full, j...  1.85 us
    unnamed x2, local copies, waits for them, and re-layouts  0.73 us

profile of v4, /device:TPU:0, one launch (start us, length us, event | category | flops | bytes accessed | tf_op | source)
XLA Modules:
  0.0 30.1 jit_solution(6163019447361941179)
XLA Ops:
  0.6 26.9 %shard_map.103.held_ref = bf16[768,256]{1,0:T(8,128)(2,1)S(1)} custom-call(bf16[256,256]{1,0:T(8,128)(2,1)} %feat_hbm.1, s32[10,256]{1,0:T(8,128)} %bitcast.2, s32[16,16]{1,0:T(8,128)} %rows_hbm.1, s32[1,16]{1,0:T(1,128)} %bitcast.3, s32[1,4]{1,0:T(1,128)} %hubs_hbm.1, bf16[256,256]{1,0:T(8,128)(2,1)} %wself_hbm.1, bf16[256,256]{1,0:T(8,128)(2,1)} %wnbr_hbm.1, ...), custom_call_target="tpu_custom_call" | custom-call | tf_op jit(solution)/shard_map/pallas_call | solution.py:438
  27.5 0.0 copy-start
  27.5 0.7 %copy-done = bf16[768,256]{1,0:T(8,128)(2,1)} copy-done((bf16[768,256]{1,0:T(8,128)(2,1)}, bf16[768,256]{1,0:T(8,128)(2,1)S(1)}, u32[]{:S(2)}) %copy-start) | copy-done | bytes 393240
  28.3 1.9 %shard_map.104 = (f32[256,256]{1,0:T(8,128)}, f32[256,256]{1,0:T(8,128)}, bf16[256,256]{1,0:T(8,128)(2,1)}) custom-call(bf16[768,256]{1,0:T(8,128)(2,1)} %copy-done), custom_call_target="tpu_custom_call" | custom-call | tf_op jit(solution)/shard_map/pallas_call | solution.py:489
Async XLA Ops:
  27.5 0.7 %copy-start = (bf16[768,256]{1,0:T(8,128)(2,1)}, bf16[768,256]{1,0:T(8,128)(2,1)S(1)}, u32[]{:S(2)}) copy-start(bf16[768,256]{1,0:T(8,128)(2,1)S(1)} %shard_map.103.held_ref) | copy-start | bytes 1179652

commit v5 on v4

--- a/solution.py
+++ b/solution.py
@@ -12,7 +12,7 @@
 BF = jnp.bfloat16
 F32 = jnp.float32
 CHUNK = 256
-CUTS = 4
+CUTS = 2
 BORDER, HUB_LINE, HUB_NEAR, BACK_BORDER, BACK_NEAR, BACK_LINE = range(6)
 SCATTER, CROSS, GATHER = 6, 6 + CUTS, 6 + 2 * CUTS
 SEMS = 6 + 3 * CUTS
@@ -108,6 +108,7 @@
     mine,
     across,
     reduced,
+    landed,
     send_sem,
     recv_sem,
 ):
@@ -149,7 +150,10 @@
         lax.fori_loop(1, count, lambda step, carry: (body(step), carry)[1], 0, unroll=count <= 16)
 
     def member(step):
-        peer = lax.rem(m + step, n_member)
+        down, up = n_member - step, step - 1
+        down = jnp.where(down > m, down, down - 1)
+        up = jnp.where(up < m, up, up + 1)
+        peer = jnp.where(m < n_member // 2, down, up)
         return peer, (g, peer)
 
     def near(step):
@@ -302,11 +306,10 @@
         scatter(per + which)
 
     dagg = dot_nt(dpre, wnbr_ref[...]) * (1.0 / fan)
-    dagg_high, dagg_low = split(dagg)
+    dagg = dagg.astype(BF)
 
     def spread(start, stop):
-        held = onehot[start:stop, :]
-        return dot(held, dagg_high) + dot(held, dagg_low)
+        return dot(onehot[start:stop, :], dagg)
 
     hub_wide = spread(hub_base, hub_base + owners * hub2)
     hub_wide = jnp.where(hub_half, hub_wide[:, :half], hub_wide[:, half:])
@@ -364,8 +367,8 @@
         source = reduced.at[pl.ds(which * piece, piece)]
         source[...] = summed.astype(BF)
         slot = rows(which * n_q + q, piece)
-        loop(n_q, lambda step: copy(source, out_ref.at[slot], GATHER + which, near(step)[1]))
-        out_ref[slot, :] = source[...]
+        loop(n_q, lambda step: copy(source, landed.at[slot], GATHER + which, near(step)[1]))
+        landed[slot, :] = source[...]
 
     for which in range(CUTS):
         gather(which)
@@ -387,7 +390,7 @@
         ],
         axis=0,
     ).astype(BF)
-    out_ref[2 * width :, :] = (total + dot(pick[:, border_rows:], hub_back)).astype(BF)
+    out_ref[2 * width :, :] = 2.0 * (total + dot(pick[:, border_rows:], hub_back))
 
     wait_bytes(out_border.at[pl.ds(0, others)], send_sem.at[BORDER])
     wait_bytes(line_hub.at[pl.ds(0, n_hi - 1)], send_sem.at[HUB_LINE])
@@ -399,21 +402,10 @@
         wait_bytes(part.at[pl.ds(which * cut, near_rows)], send_sem.at[SCATTER + which])
         wait_bytes(across.at[pl.ds(which * n_hi * piece, line_rows)], send_sem.at[CROSS + which])
     for which in range(CUTS):
-        wait_bytes(out_ref.at[pl.ds(which * cut, near_rows)], recv_sem.at[GATHER + which])
+        wait_bytes(landed.at[pl.ds(which * cut, near_rows)], recv_sem.at[GATHER + which])
+        span = slice(which * cut, (which + 1) * cut)
+        out_ref[span, :] = landed[span, :].astype(F32)
         wait_bytes(part.at[pl.ds(which * cut, near_rows)], send_sem.at[GATHER + which])
-
-
-def finish(scale, held_ref, self_hbm, nbr_hbm, feat_hbm, stage, sems):
-    width = stage.shape[0] // 2
-    copies = [pltpu.make_async_copy(held_ref.at[pl.ds(2 * width, feat_hbm.shape[0])], feat_hbm, sems.at[2])]
-    copies[0].start()
-    for index, target in enumerate((self_hbm, nbr_hbm)):
-        span = pl.ds(index * width, width)
-        stage[span, :] = held_ref[span, :].astype(F32) * scale
-        copies.append(pltpu.make_async_copy(stage.at[span], target, sems.at[index]))
-        copies[-1].start()
-    for copy in copies:
-        copy.wait()
 
 
 def local(features, neighbours, send_rows, block_counts, hub_rows, w_self, w_nbr, cotangent):
@@ -437,7 +429,7 @@
     pair = pltpu.VMEM((2 * width, width), BF)
     result = pl.pallas_call(
         functools.partial(kernel, n_group, n_member, low, block, hubs),
-        out_shape=pltpu.VMEM((2 * width + nodes, width), BF),
+        out_shape=pltpu.VMEM((2 * width + nodes, width), F32),
         in_specs=[pl.BlockSpec(memory_space=pltpu.HBM)] * 8,
         out_specs=pl.BlockSpec(memory_space=pltpu.VMEM),
         scratch_shapes=[
@@ -468,6 +460,7 @@
             pltpu.VMEM((CUTS * piece, width), BF),
             pltpu.VMEM((CUTS * n_hi * piece, width), BF),
             pltpu.VMEM((CUTS * piece, width), BF),
+            pair,
             pltpu.SemaphoreType.DMA((SEMS,)),
             pltpu.SemaphoreType.DMA((SEMS,)),
         ],
@@ -485,14 +478,9 @@
         cotangent,
     )
     scale = 1.0 / math.sqrt(nodes * owners)
-    full = jax.ShapeDtypeStruct((width, width), F32)
-    return pl.pallas_call(
-        functools.partial(finish, scale),
-        out_shape=(full, full, jax.ShapeDtypeStruct((nodes, width), BF)),
-        in_specs=[pl.BlockSpec(memory_space=pltpu.VMEM)],
-        out_specs=(pl.BlockSpec(memory_space=pl.ANY),) * 3,
-        scratch_shapes=[pltpu.VMEM((2 * width, width), F32), pltpu.SemaphoreType.DMA((3,))],
-    )(result)
+    grad_self = result[:width] * scale
+    grad_nbr = result[width : 2 * width] * scale
+    return (grad_self, grad_nbr, (0.5 * result[2 * width :]).astype(BF))
 
 
 def solution(mesh):

time: 30.3 us -> 28.9 us (0.954)
  Pallas kernels: 28.7 us -> 27.2 us
  other arithmetic: 0 us -> 0.86 us
  local copies, waits for them, and re-layouts: 0.73 us -> 0 us
    pallas_call x1 -> x0, Pallas kernels: 1.85 us -> none  [local(): pl.pallas_call(functools.partial(finish, scale), out_shape=(full, full, j...]
    convert_element_type x0 -> x1, other arithmetic: none -> 0.86 us  [local(): return (grad_self, grad_nbr, (0.5 * result[2 * width:]).astype(BF))]
    unnamed x2 -> x0, local copies, waits for them, and re-layouts: 0.73 us -> none
    pallas_call x1, Pallas kernels: 26.9 us -> 27.2 us  [local(): pl.pallas_call(functools.partial(kernel, n_group, n_member, low, block, h...]
where the time goes in v5:
time: 28.9 us; the launch traced here: 28.7 us
  Pallas kernels  27.2 us (94%)
  other arithmetic  0.86 us (3%)
  between operations  0.64 us (2%)
    pallas_call x1, Pallas kernels, local(): pl.pallas_call(functools.partial(kernel, n_group, n_member, low, block, h...  27.2 us
    convert_element_type x1, other arithmetic, local(): return (grad_self, grad_nbr, (0.5 * result[2 * width:]).astype(BF))  0.86 us

profile of v5, /device:TPU:0, one launch (start us, length us, event | category | flops | bytes accessed | tf_op | source)
XLA Modules:
  0.0 28.7 jit_solution(10889856068966903579)
XLA Ops:
  0.6 27.2 %shard_map.103 = f32[768,256]{1,0:T(8,128)S(1)} custom-call(bf16[256,256]{1,0:T(8,128)(2,1)} %feat_hbm.1, s32[10,256]{1,0:T(8,128)} %bitcast.2, s32[16,16]{1,0:T(8,128)} %rows_hbm.1, s32[1,16]{1,0:T(1,128)} %bitcast.3, s32[1,4]{1,0:T(1,128)} %hubs_hbm.1, bf16[256,256]{1,0:T(8,128)(2,1)} %wself_hbm.1, bf16[256,256]{1,0:T(8,128)(2,1)} %wnbr_hbm.1, ...), custom_call_target="tpu_custom_call" | custom-call | tf_op jit(solution)/shard_map/pallas_call | solution.py:430
  27.8 0.9 %multiply_convert_fusion = (bf16[256,256]{1,0:T(8,128)(2,1)}, f32[256,256]{1,0:T(8,128)}, f32[256,256]{1,0:T(8,128)}) fusion(f32[768,256]{1,0:T(8,128)S(1)} %shard_map.103), kind=kLoop, calls=%fused_computation | loop fusion | flops 262144 | bytes 1441792 | tf_op jit(solution)/shard_map/convert_element_type | solution.py:483

commit v6 on v5

--- a/solution.py
+++ b/solution.py
@@ -11,7 +11,7 @@
 MESH = pl.DeviceIdType.MESH
 BF = jnp.bfloat16
 F32 = jnp.float32
-CHUNK = 256
+CHUNK = 128
 CUTS = 2
 BORDER, HUB_LINE, HUB_NEAR, BACK_BORDER, BACK_NEAR, BACK_LINE = range(6)
 SCATTER, CROSS, GATHER = 6, 6 + CUTS, 6 + 2 * CUTS
@@ -147,7 +147,7 @@
         load.start()
 
     def loop(count, body):
-        lax.fori_loop(1, count, lambda step, carry: (body(step), carry)[1], 0, unroll=count <= 16)
+        lax.fori_loop(1, count, lambda step, carry: (body(step), carry)[1], 0)
 
     def member(step):
         down, up = n_member - step, step - 1
@@ -232,31 +232,26 @@
         onehot[rows(index, CHUNK), :] = total.astype(BF)
         onehot_t[:, rows(index, CHUNK)] = total.T.astype(BF)
 
-    plain_chunks = hub_base // CHUNK
-    hub_chunks = owners * hub2 // CHUNK
-
-    def fill_plain(index, carry):
-        store(index, count(chunk_names(index)))
-        return carry
-
-    def fill_hub(index, carry):
+    def fill(index, carry):
         row = chunk_names(index)
-        slab = lax.div(row, hub2)
+        hub_row = row - hub_base
+        slab = lax.div(hub_row, hub2)
         near_id = lax.div(slab, n_hi)
         owner = (
             lax.div(near_id, low) * n_member + lax.rem(slab, n_hi) * low + lax.rem(near_id, low)
         )
-        store(plain_chunks + index, count(hub_base + owner * hubs + lax.rem(row, hubs)))
+        hub_name = hub_base + owner * hubs + lax.rem(hub_row, hubs)
+        store(index, count(jnp.where(row < hub_base, row, hub_name)))
         return carry
 
-    fill_plain(0, 0)
+    early = nodes // CHUNK
+    lax.fori_loop(0, early, fill, 0)
 
     wait_bytes(line_hub.at[pl.ds(0, n_hi - 1)], recv_sem.at[HUB_LINE])
     loop(n_q, lambda step: copy(line_hub, in_hub.at[q], HUB_NEAR, near(step)[1]))
     in_hub[q] = line_hub[...]
 
-    lax.fori_loop(1, plain_chunks, fill_plain, 0)
-    lax.fori_loop(0, hub_chunks, fill_hub, 0)
+    lax.fori_loop(early, onehot.shape[0] // CHUNK, fill, 0)
     pre_self = dot(feat, wself_ref[...])
     agg_sum = dot(onehot_t[:, :nodes], feat)
     feat_t = feat.astype(F32).T.astype(BF)

time: 28.9 us -> 28.9 us (level)
  no operation moved by 1% of the time
where the time goes in v6:
time: 28.9 us; the launch traced here: 28.7 us
  Pallas kernels  27.2 us (94%)
  other arithmetic  0.86 us (3%)
  between operations  0.64 us (2%)
    pallas_call x1, Pallas kernels, local(): pl.pallas_call(functools.partial(kernel, n_group, n_member, low, block, h...  27.2 us
    convert_element_type x1, other arithmetic, local(): return (grad_self, grad_nbr, (0.5 * result[2 * width:]).astype(BF))  0.86 us

profile of v6, /device:TPU:0, one launch (start us, length us, event | category | flops | bytes accessed | tf_op | source)
XLA Modules:
  0.0 28.7 jit_solution(13404488051654343398)
XLA Ops:
  0.6 27.2 %shard_map.103 = f32[768,256]{1,0:T(8,128)S(1)} custom-call(bf16[256,256]{1,0:T(8,128)(2,1)} %feat_hbm.1, s32[10,256]{1,0:T(8,128)} %bitcast.2, s32[16,16]{1,0:T(8,128)} %rows_hbm.1, s32[1,16]{1,0:T(1,128)} %bitcast.3, s32[1,4]{1,0:T(1,128)} %hubs_hbm.1, bf16[256,256]{1,0:T(8,128)(2,1)} %wself_hbm.1, bf16[256,256]{1,0:T(8,128)(2,1)} %wnbr_hbm.1, ...), custom_call_target="tpu_custom_call" | custom-call | tf_op jit(solution)/shard_map/pallas_call | solution.py:425
  27.8 0.9 %multiply_convert_fusion = (bf16[256,256]{1,0:T(8,128)(2,1)}, f32[256,256]{1,0:T(8,128)}, f32[256,256]{1,0:T(8,128)}) fusion(f32[768,256]{1,0:T(8,128)S(1)} %shard_map.103), kind=kLoop, calls=%fused_computation | loop fusion | flops 262144 | bytes 1441792 | tf_op jit(solution)/shard_map/convert_element_type | solution.py:478

commit v7 on v6

--- a/solution.py
+++ b/solution.py
@@ -292,6 +292,15 @@
         span = slice(which * cut, (which + 1) * cut)
         part[span, :] = dot(feat_t[span, :], dpre).astype(BF)
         scatter(which)
+    dagg = dot_nt(dpre, wnbr_ref[...]) * (1.0 / fan)
+    dagg = dagg.astype(BF)
+
+    def spread(start, stop):
+        return dot(onehot[start:stop, :], dagg)
+
+    back_border[...] = spread(nodes, hub_base).astype(BF)
+    to_members(back_border, ret_border, BACK_BORDER)
+
     agg_t = agg.astype(F32).T.astype(BF)
     for which in range(per):
         span = slice(which * cut, (which + 1) * cut)
@@ -300,12 +309,6 @@
         ).astype(BF)
         scatter(per + which)
 
-    dagg = dot_nt(dpre, wnbr_ref[...]) * (1.0 / fan)
-    dagg = dagg.astype(BF)
-
-    def spread(start, stop):
-        return dot(onehot[start:stop, :], dagg)
-
     hub_wide = spread(hub_base, hub_base + owners * hub2)
     hub_wide = jnp.where(hub_half, hub_wide[:, :half], hub_wide[:, half:])
     back_hub[...] = hub_wide.reshape(n_q, n_hi, hub2, half).astype(BF)
@@ -316,8 +319,6 @@
 
     loop(n_q, send_back)
     ret_hub[q] = back_hub[q]
-    back_border[...] = spread(nodes, hub_base).astype(BF)
-    to_members(back_border, ret_border, BACK_BORDER)
 
     near_rows = (n_q - 1) * piece
     line_rows = (n_hi - 1) * piece

time: 28.9 us -> 29.1 us (level)
  no operation moved by 1% of the time
where the time goes in v7:
time: 29.1 us; the launch traced here: 28.9 us
  Pallas kernels  27.4 us (94%)
  other arithmetic  0.86 us (3%)
  between operations  0.64 us (2%)
    pallas_call x1, Pallas kernels, local(): pl.pallas_call(functools.partial(kernel, n_group, n_member, low, block, h...  27.4 us
    convert_element_type x1, other arithmetic, local(): return (grad_self, grad_nbr, (0.5 * result[2 * width:]).astype(BF))  0.86 us

profile of v7, /device:TPU:0, one launch (start us, length us, event | category | flops | bytes accessed | tf_op | source)
XLA Modules:
  0.0 28.9 jit_solution(11363799356662220332)
XLA Ops:
  0.6 27.4 %shard_map.103 = f32[768,256]{1,0:T(8,128)S(1)} custom-call(bf16[256,256]{1,0:T(8,128)(2,1)} %feat_hbm.1, s32[10,256]{1,0:T(8,128)} %bitcast.2, s32[16,16]{1,0:T(8,128)} %rows_hbm.1, s32[1,16]{1,0:T(1,128)} %bitcast.3, s32[1,4]{1,0:T(1,128)} %hubs_hbm.1, bf16[256,256]{1,0:T(8,128)(2,1)} %wself_hbm.1, bf16[256,256]{1,0:T(8,128)(2,1)} %wnbr_hbm.1, ...), custom_call_target="tpu_custom_call" | custom-call | tf_op jit(solution)/shard_map/pallas_call | solution.py:426
  28.0 0.9 %multiply_convert_fusion = (bf16[256,256]{1,0:T(8,128)(2,1)}, f32[256,256]{1,0:T(8,128)}, f32[256,256]{1,0:T(8,128)}) fusion(f32[768,256]{1,0:T(8,128)S(1)} %shard_map.103), kind=kLoop, calls=%fused_computation | loop fusion | flops 262144 | bytes 1441792 | tf_op jit(solution)/shard_map/convert_element_type | solution.py:479

commit v8 on v6

--- a/solution.py
+++ b/solution.py
@@ -12,10 +12,9 @@
 BF = jnp.bfloat16
 F32 = jnp.float32
 CHUNK = 128
-CUTS = 2
 BORDER, HUB_LINE, HUB_NEAR, BACK_BORDER, BACK_NEAR, BACK_LINE = range(6)
-SCATTER, CROSS, GATHER = 6, 6 + CUTS, 6 + 2 * CUTS
-SEMS = 6 + 3 * CUTS
+SCATTER, CROSS, GATHER = 6, 8, 10
+SEMS = 12
 
 
 def dot(a, b):
@@ -70,6 +69,7 @@
     n_group,
     n_member,
     low,
+    cuts,
     block,
     hubs,
     feat_hbm,
@@ -125,7 +125,7 @@
     n_hi = n_member // low
     n_q = n_group * low
     q = g * low + lo
-    piece = 2 * width // (CUTS * n_q)
+    piece = 2 * width // (cuts * n_q)
     cut = n_q * piece
 
     loads = [
@@ -247,7 +247,8 @@
     early = nodes // CHUNK
     lax.fori_loop(0, early, fill, 0)
 
-    wait_bytes(line_hub.at[pl.ds(0, n_hi - 1)], recv_sem.at[HUB_LINE])
+    if n_hi > 1:
+        wait_bytes(line_hub.at[pl.ds(0, n_hi - 1)], recv_sem.at[HUB_LINE])
     loop(n_q, lambda step: copy(line_hub, in_hub.at[q], HUB_NEAR, near(step)[1]))
     in_hub[q] = line_hub[...]
 
@@ -287,18 +288,11 @@
         own = rows(which * n_q + q, piece)
         scattered[own, :] = part[own, :]
 
-    per = width // cut
-    for which in range(per):
-        span = slice(which * cut, (which + 1) * cut)
-        part[span, :] = dot(feat_t[span, :], dpre).astype(BF)
-        scatter(which)
-    agg_t = agg.astype(F32).T.astype(BF)
-    for which in range(per):
-        span = slice(which * cut, (which + 1) * cut)
-        part[width + which * cut : width + (which + 1) * cut, :] = dot(
-            agg_t[span, :], dpre
-        ).astype(BF)
-        scatter(per + which)
+    part[:width, :] = dot(feat_t, dpre).astype(BF)
+    if cuts == 2:
+        scatter(0)
+    part[width:, :] = dot_tn(agg, dpre).astype(BF)
+    scatter(cuts - 1)
 
     dagg = dot_nt(dpre, wnbr_ref[...]) * (1.0 / fan)
     dagg = dagg.astype(BF)
@@ -334,7 +328,7 @@
         loop(n_hi, lambda step: copy(source, across.at[slot], CROSS + which, line(step)[1]))
         across[slot, :] = source[...]
 
-    for which in range(CUTS):
+    for which in range(cuts):
         cross(which)
 
     total = dot_nt(dpre, wself_ref[...]) + spread(0, nodes)
@@ -351,7 +345,8 @@
 
     def gather(which):
         first = which * n_hi
-        wait_bytes(across.at[pl.ds(first * piece, line_rows)], recv_sem.at[CROSS + which])
+        if n_hi > 1:
+            wait_bytes(across.at[pl.ds(first * piece, line_rows)], recv_sem.at[CROSS + which])
         summed = lax.fori_loop(
             0,
             n_hi,
@@ -365,12 +360,13 @@
         loop(n_q, lambda step: copy(source, landed.at[slot], GATHER + which, near(step)[1]))
         landed[slot, :] = source[...]
 
-    for which in range(CUTS):
+    for which in range(cuts):
         gather(which)
 
     wait_bytes(ret_border.at[pl.ds(0, others)], recv_sem.at[BACK_BORDER])
     total = total + dot(pick[:, :border_rows], ret_border[...])
-    wait_bytes(line_ret.at[pl.ds(0, n_hi - 1)], recv_sem.at[BACK_LINE])
+    if n_hi > 1:
+        wait_bytes(line_ret.at[pl.ds(0, n_hi - 1)], recv_sem.at[BACK_LINE])
     hub_sum = jnp.sum(line_ret[...].astype(F32), axis=0)
     top = lane_row < hubs
     hub_sum = jnp.concatenate(
@@ -388,15 +384,20 @@
     out_ref[2 * width :, :] = 2.0 * (total + dot(pick[:, border_rows:], hub_back))
 
     wait_bytes(out_border.at[pl.ds(0, others)], send_sem.at[BORDER])
-    wait_bytes(line_hub.at[pl.ds(0, n_hi - 1)], send_sem.at[HUB_LINE])
+    if n_hi > 1:
+        wait_bytes(line_hub.at[pl.ds(0, n_hi - 1)], send_sem.at[HUB_LINE])
     wait_bytes(in_hub.at[pl.ds(0, n_q - 1)], send_sem.at[HUB_NEAR])
     wait_bytes(back_border.at[pl.ds(0, others)], send_sem.at[BACK_BORDER])
     wait_bytes(back_hub.at[pl.ds(0, n_q - 1)], send_sem.at[BACK_NEAR])
-    wait_bytes(line_back.at[pl.ds(0, n_hi - 1)], send_sem.at[BACK_LINE])
-    for which in range(CUTS):
+    if n_hi > 1:
+        wait_bytes(line_back.at[pl.ds(0, n_hi - 1)], send_sem.at[BACK_LINE])
+    for which in range(cuts):
         wait_bytes(part.at[pl.ds(which * cut, near_rows)], send_sem.at[SCATTER + which])
-        wait_bytes(across.at[pl.ds(which * n_hi * piece, line_rows)], send_sem.at[CROSS + which])
-    for which in range(CUTS):
+        if n_hi > 1:
+            wait_bytes(
+                across.at[pl.ds(which * n_hi * piece, line_rows)], send_sem.at[CROSS + which]
+            )
+    for which in range(cuts):
         wait_bytes(landed.at[pl.ds(which * cut, near_rows)], recv_sem.at[GATHER + which])
         span = slice(which * cut, (which + 1) * cut)
         out_ref[span, :] = landed[span, :].astype(F32)
@@ -411,10 +412,12 @@
     hubs = hub_rows.shape[1]
     owners = n_group * n_member
     hub2 = 2 * hubs
-    low = max(1, 8 // n_group)
+    low, cuts = max(1, 8 // n_group), 2
+    if 2 * width % (16 * owners) == 0:
+        low, cuts = n_member, 1
     n_q = n_group * low
     n_hi = n_member // low
-    piece = 2 * width // (CUTS * n_q)
+    piece = 2 * width // (cuts * n_q)
     half = width // 2
     border_rows = n_member * block
     table_rows = nodes + border_rows + owners * hub2
@@ -423,7 +426,7 @@
     hub_all = pltpu.VMEM((n_q, n_hi, hub2, half), BF)
     pair = pltpu.VMEM((2 * width, width), BF)
     result = pl.pallas_call(
-        functools.partial(kernel, n_group, n_member, low, block, hubs),
+        functools.partial(kernel, n_group, n_member, low, cuts, block, hubs),
         out_shape=pltpu.VMEM((2 * width + nodes, width), F32),
         in_specs=[pl.BlockSpec(memory_space=pltpu.HBM)] * 8,
         out_specs=pl.BlockSpec(memory_space=pltpu.VMEM),
@@ -452,9 +455,9 @@
             hub_line,
             pair,
             pair,
-            pltpu.VMEM((CUTS * piece, width), BF),
-            pltpu.VMEM((CUTS * n_hi * piece, width), BF),
-            pltpu.VMEM((CUTS * piece, width), BF),
+            pltpu.VMEM((cuts * piece, width), BF),
+            pltpu.VMEM((cuts * n_hi * piece, width), BF),
+            pltpu.VMEM((cuts * piece, width), BF),
             pair,
             pltpu.SemaphoreType.DMA((SEMS,)),
             pltpu.SemaphoreType.DMA((SEMS,)),

time: 28.9 us -> 35.1 us (1.21)
  Pallas kernels: 27.2 us -> 33.4 us
    pallas_call x1, Pallas kernels: 27.2 us -> 33.4 us  [local(): pl.pallas_call(functools.partial(kernel, n_group, n_member, low, cuts, bl...]
where the time goes in v8:
time: 35.1 us; the launch traced here: 34.9 us
  Pallas kernels  33.4 us (95%)
  other arithmetic  0.86 us (2%)
  between operations  0.64 us (2%)
    pallas_call x1, Pallas kernels, local(): pl.pallas_call(functools.partial(kernel, n_group, n_member, low, cuts, bl...  33.4 us
    convert_element_type x1, other arithmetic, local(): return (grad_self, grad_nbr, (0.5 * result[2 * width:]).astype(BF))  0.86 us

profile of v8, /device:TPU:0, one launch (start us, length us, event | category | flops | bytes accessed | tf_op | source)
XLA Modules:
  0.0 34.9 jit_solution(13604776387621841232)
XLA Ops:
  0.6 33.4 %shard_map.103 = f32[768,256]{1,0:T(8,128)S(1)} custom-call(bf16[256,256]{1,0:T(8,128)(2,1)} %feat_hbm.1, s32[10,256]{1,0:T(8,128)} %bitcast.2, s32[16,16]{1,0:T(8,128)} %rows_hbm.1, s32[1,16]{1,0:T(1,128)} %bitcast.3, s32[1,4]{1,0:T(1,128)} %hubs_hbm.1, bf16[256,256]{1,0:T(8,128)(2,1)} %wself_hbm.1, bf16[256,256]{1,0:T(8,128)(2,1)} %wnbr_hbm.1, ...), custom_call_target="tpu_custom_call" | custom-call | tf_op jit(solution)/shard_map/pallas_call | solution.py:428
  34.0 0.9 %multiply_convert_fusion = (bf16[256,256]{1,0:T(8,128)(2,1)}, f32[256,256]{1,0:T(8,128)}, f32[256,256]{1,0:T(8,128)}) fusion(f32[768,256]{1,0:T(8,128)S(1)} %shard_map.103), kind=kLoop, calls=%fused_computation | loop fusion | flops 262144 | bytes 1441792 | tf_op jit(solution)/shard_map/convert_element_type | solution.py:481

commit v9 on v6

--- a/solution.py
+++ b/solution.py
@@ -108,7 +108,6 @@
     mine,
     across,
     reduced,
-    landed,
     send_sem,
     recv_sem,
 ):
@@ -362,8 +361,8 @@
         source = reduced.at[pl.ds(which * piece, piece)]
         source[...] = summed.astype(BF)
         slot = rows(which * n_q + q, piece)
-        loop(n_q, lambda step: copy(source, landed.at[slot], GATHER + which, near(step)[1]))
-        landed[slot, :] = source[...]
+        loop(n_q, lambda step: copy(source, out_ref.at[slot], GATHER + which, near(step)[1]))
+        out_ref[slot, :] = source[...]
 
     for which in range(CUTS):
         gather(which)
@@ -385,7 +384,9 @@
         ],
         axis=0,
     ).astype(BF)
-    out_ref[2 * width :, :] = 2.0 * (total + dot(pick[:, border_rows:], hub_back))
+    out_ref[2 * width :, :] = (
+        2.0 * (total + dot(pick[:, border_rows:], hub_back))
+    ).astype(BF)
 
     wait_bytes(out_border.at[pl.ds(0, others)], send_sem.at[BORDER])
     wait_bytes(line_hub.at[pl.ds(0, n_hi - 1)], send_sem.at[HUB_LINE])
@@ -397,9 +398,7 @@
         wait_bytes(part.at[pl.ds(which * cut, near_rows)], send_sem.at[SCATTER + which])
         wait_bytes(across.at[pl.ds(which * n_hi * piece, line_rows)], send_sem.at[CROSS + which])
     for which in range(CUTS):
-        wait_bytes(landed.at[pl.ds(which * cut, near_rows)], recv_sem.at[GATHER + which])
-        span = slice(which * cut, (which + 1) * cut)
-        out_ref[span, :] = landed[span, :].astype(F32)
+        wait_bytes(out_ref.at[pl.ds(which * cut, near_rows)], recv_sem.at[GATHER + which])
         wait_bytes(part.at[pl.ds(which * cut, near_rows)], send_sem.at[GATHER + which])
 
 
@@ -424,7 +423,7 @@
     pair = pltpu.VMEM((2 * width, width), BF)
     result = pl.pallas_call(
         functools.partial(kernel, n_group, n_member, low, block, hubs),
-        out_shape=pltpu.VMEM((2 * width + nodes, width), F32),
+        out_shape=pltpu.VMEM((2 * width + nodes, width), BF),
         in_specs=[pl.BlockSpec(memory_space=pltpu.HBM)] * 8,
         out_specs=pl.BlockSpec(memory_space=pltpu.VMEM),
         scratch_shapes=[
@@ -455,7 +454,6 @@
             pltpu.VMEM((CUTS * piece, width), BF),
             pltpu.VMEM((CUTS * n_hi * piece, width), BF),
             pltpu.VMEM((CUTS * piece, width), BF),
-            pair,
             pltpu.SemaphoreType.DMA((SEMS,)),
             pltpu.SemaphoreType.DMA((SEMS,)),
         ],
@@ -473,9 +471,10 @@
         cotangent,
     )
     scale = 1.0 / math.sqrt(nodes * owners)
-    grad_self = result[:width] * scale
-    grad_nbr = result[width : 2 * width] * scale
-    return (grad_self, grad_nbr, (0.5 * result[2 * width :]).astype(BF))
+    grad_self = result[:width].astype(F32) * scale
+    grad_nbr = result[width : 2 * width].astype(F32) * scale
+    grad_feat = (result[2 * width :].astype(F32) * 0.5).astype(BF)
+    return (grad_self, grad_nbr, grad_feat)
 
 
 def solution(mesh):

time: 28.9 us -> 28.9 us (level)
  no operation moved by 1% of the time
where the time goes in v9:
time: 28.9 us; the launch traced here: 28.6 us
  Pallas kernels  27.2 us (94%)
  other arithmetic  0.85 us (3%)
  between operations  0.64 us (2%)
    pallas_call x1, Pallas kernels, local(): pl.pallas_call(functools.partial(kernel, n_group, n_member, low, block, h...  27.2 us
    convert_element_type x1, other arithmetic, local(): grad_feat = (result[2 * width:].astype(F32) * 0.5).astype(BF)  0.85 us

profile of v9, /device:TPU:0, one launch (start us, length us, event | category | flops | bytes accessed | tf_op | source)
XLA Modules:
  0.0 28.6 jit_solution(15014870478749909196)
XLA Ops:
  0.6 27.2 %shard_map.103 = bf16[768,256]{1,0:T(8,128)(2,1)S(1)} custom-call(bf16[256,256]{1,0:T(8,128)(2,1)} %feat_hbm.1, s32[10,256]{1,0:T(8,128)} %bitcast.2, s32[16,16]{1,0:T(8,128)} %rows_hbm.1, s32[1,16]{1,0:T(1,128)} %bitcast.3, s32[1,4]{1,0:T(1,128)} %hubs_hbm.1, bf16[256,256]{1,0:T(8,128)(2,1)} %wself_hbm.1, bf16[256,256]{1,0:T(8,128)(2,1)} %wnbr_hbm.1, ...), custom_call_target="tpu_custom_call" | custom-call | tf_op jit(solution)/shard_map/pallas_call | solution.py:424
  27.8 0.9 %multiply_convert_fusion = (bf16[256,256]{1,0:T(8,128)(2,1)}, f32[256,256]{1,0:T(8,128)}, f32[256,256]{1,0:T(8,128)}) fusion(bf16[768,256]{1,0:T(8,128)(2,1)S(1)} %shard_map.103), kind=kLoop, calls=%fused_computation | loop fusion | flops 458752 | bytes 1048576 | tf_op jit(solution)/shard_map/convert_element_type | solution.py:476

commit v10 on v8

--- a/solution.py
+++ b/solution.py
@@ -412,9 +412,7 @@
     hubs = hub_rows.shape[1]
     owners = n_group * n_member
     hub2 = 2 * hubs
-    low, cuts = max(1, 8 // n_group), 2
-    if 2 * width % (16 * owners) == 0:
-        low, cuts = n_member, 1
+    low, cuts = max(1, 8 // n_group), 1
     n_q = n_group * low
     n_hi = n_member // low
     piece = 2 * width // (cuts * n_q)

time: 35.1 us -> 29.7 us (0.85)
  Pallas kernels: 33.4 us -> 28 us
    pallas_call x1, Pallas kernels: 33.4 us -> 28 us  [local(): pl.pallas_call(functools.partial(kernel, n_group, n_member, low, cuts, bl...]
where the time goes in v10:
time: 29.7 us; the launch traced here: 29.5 us
  Pallas kernels  28 us (94%)
  other arithmetic  0.86 us (3%)
  between operations  0.64 us (2%)
    pallas_call x1, Pallas kernels, local(): pl.pallas_call(functools.partial(kernel, n_group, n_member, low, cuts, bl...  28 us
    convert_element_type x1, other arithmetic, local(): return (grad_self, grad_nbr, (0.5 * result[2 * width:]).astype(BF))  0.86 us

profile of v10, /device:TPU:0, one launch (start us, length us, event | category | flops | bytes accessed | tf_op | source)
XLA Modules:
  0.0 29.5 jit_solution(8780423469724645322)
XLA Ops:
  0.6 28.0 %shard_map.103 = f32[768,256]{1,0:T(8,128)S(1)} custom-call(bf16[256,256]{1,0:T(8,128)(2,1)} %feat_hbm.1, s32[10,256]{1,0:T(8,128)} %bitcast.2, s32[16,16]{1,0:T(8,128)} %rows_hbm.1, s32[1,16]{1,0:T(1,128)} %bitcast.3, s32[1,4]{1,0:T(1,128)} %hubs_hbm.1, bf16[256,256]{1,0:T(8,128)(2,1)} %wself_hbm.1, bf16[256,256]{1,0:T(8,128)(2,1)} %wnbr_hbm.1, ...), custom_call_target="tpu_custom_call" | custom-call | tf_op jit(solution)/shard_map/pallas_call | solution.py:426
  28.6 0.9 %multiply_convert_fusion = (bf16[256,256]{1,0:T(8,128)(2,1)}, f32[256,256]{1,0:T(8,128)}, f32[256,256]{1,0:T(8,128)}) fusion(f32[768,256]{1,0:T(8,128)S(1)} %shard_map.103), kind=kLoop, calls=%fused_computation | loop fusion | flops 262144 | bytes 1441792 | tf_op jit(solution)/shard_map/convert_element_type | solution.py:479
